TPU v7x, 1024 devices: a whole 4x8x16 slice. The times are simulated.
1024 devices in a mesh: dp: 64 (over z_hi, y, core), tensor: 16 (over z_lo, x).
Axes of the slice: x: 4, y: 8, z: 16 (z_hi: 4, z_lo: 4; z = z_hi * 4 + z_lo), core: 2. Of those that a mesh axis runs over, the one named last changes fastest.
Arguments:
- gate_pre: bfloat16 [32768, 14336], P(('dp', 'tensor')), parts along dimension 0, may hold values from -6 to 6
- up_pre: bfloat16 [32768, 14336], P(('dp', 'tensor')), parts along dimension 0, may hold values from -6 to 6
- down_weight: bfloat16 [14336, 4096], P('tensor'), may hold values from -0.046875 to 0.046875
Outputs:
- mixed: bfloat16 [32768, 4096], P(('dp', 'tensor')), parts along dimension 0
There are 64 independent parts, one for each index of `dp`. A program takes and returns all parts, laid end to end along the dimension named above; an argument that names none is the same for every part. Nothing has to cross between parts.
All inputs are finite; a program needn't handle non-finite values.
Results may differ from a plain program's by a relative error of at most 0.023.
Values may be sent and summed in bfloat16 or wider, within the bound.
No kernel may reach another device: no remote copies, remote signals or barrier semaphores. Data moves between devices by JAX's collectives and lax.ppermute only.
A program may use at most 32 MiB of HBM per device.

v0:
```python
import jax
import jax.numpy as jnp
from jax import lax
from jax.sharding import PartitionSpec as P


def activate(gate_vals, up_vals):
    return (jax.nn.silu(gate_vals.astype(jnp.float32)) * up_vals.astype(jnp.float32)).astype(
        jnp.bfloat16
    )


def shards(gate_pre, up_pre, down_weight):
    hidden_local = activate(gate_pre, up_pre)
    hidden = lax.all_to_all(hidden_local, "tensor", split_axis=1, concat_axis=0, tiled=True)
    terms = jnp.dot(hidden, down_weight, preferred_element_type=jnp.float32)
    summed = lax.psum_scatter(terms.astype(jnp.bfloat16), "tensor", scatter_dimension=0, tiled=True)
    return summed


def solution(mesh):
    return jax.shard_map(
        shards,
        mesh=mesh,
        in_specs=(P(("dp", "tensor"), None), P(("dp", "tensor"), None), P("tensor", None)),
        out_specs=P(("dp", "tensor"), None),
        check_vma=False,
    )
```

profile of v0, /device:TPU:56, one launch (start us, length us, event | category | flops | bytes accessed | tf_op | source)
XLA Modules:
  0.0 164.2 jit_solution(15140113991218249654)
XLA Ops:
  6.5 0.0 reduce-scatter.2.cloned.1.call-start
  6.5 2.0 %fusion.4 = bf16[32,14336]{1,0:T(8,128)(2,1)S(1)} fusion(bf16[32,14336]{1,0:T(8,128)(2,1)} %param.4, bf16[32,14336]{1,0:T(8,128)(2,1)} %param.3), kind=kLoop, calls=%fused_computation.7 | loop fusion | flops 3670016 | bytes 2752512 | tf_op jit(solution)/shard_map/convert_element_type | solution.py:8
  8.5 0.1 copy.8
  8.6 33.8 %all_to_all.19 = bf16[32,16,896]{2,0,1:T(8,128)(2,1)S(1)} all-to-all(bf16[32,16,896]{2,0,1:T(8,128)(2,1)S(1)} %bitcast.9), channel_id=1, replica_groups=mesh['dp'=64,'tensor'=16] {'tensor'}, dimensions={1} | all-to-all | bytes 1835008 | tf_op jit(solution)/shard_map/all_to_all | solution.py:15
  42.4 9.2 %convolution_convert_fusion = bf16[512,4096]{1,0:T(8,128)(2,1)} fusion(bf16[512,896]{1,0:T(8,128)(2,1)S(1)} %bitcast.11, bf16[896,4096]{1,0:T(8,128)(2,1)} %param.5), kind=kOutput, calls=%fused_computation | convolution fusion | flops 3760193536 | bytes 12451840 | tf_op jit(solution)/shard_map/dot_general | solution.py:16
  51.6 0.0 reduce-scatter.2.cloned.1.call-update
  51.6 105.7 %reduce-scatter.2.cloned.1.call-done = bf16[32,4096]{1,0:T(8,128)(2,1)} async-done(((bf16[512,4096]{1,0:T(8,128)(2,1)}), bf16[32,4096]{1,0:T(8,128)(2,1)}) %reduce-scatter.2.cloned.1.call-update) | async-done | bytes 262160 | tf_op jit(solution)/shard_map/reduce_scatter | solution.py:17
Async XLA Ops:
  6.5 150.8 %reduce-scatter.2.cloned.1.call-start = ((), (), s32[]{:S(2)}) async-start(), calls=%async_computation.2 | async-start | bytes 4456448 | tf_op jit(solution)/shard_map/reduce_scatter | solution.py:17
Sparse Core Ops, SparseCore 0:
  51.7 105.5 reduce-scatter.1
where the time goes:
time: 165 us; the launch traced here: 164 us
  waiting for transfers between devices  106 us (64%)
  blocking collectives  33.8 us (20%)
  between operations  13.4 us (8%)
  matrix products  9.21 us (6%)
  other arithmetic  1.97 us (1%)
    reduce_scatter x1, waiting for transfers between devices, shards(): lax.psum_scatter(terms.astype(jnp.bfloat16), 'tensor', scatter_dimension=...  106 us
    all_to_all x1, blocking collectives, shards(): lax.all_to_all(hidden_local, 'tensor', split_axis=1, concat_axis=0, tiled...  33.8 us
    dot_general x1, matrix products, shards(): terms = jnp.dot(hidden, down_weight, preferred_element_type=jnp.float32)  9.21 us
  transfers between devices with their start and end apart: 1, of which 1 were waited for; matrix products, arithmetic and copies ran while one was open for 0% of the time, Pallas kernels for 0%

commit v1 on v0

v1 whole, which is shorter than its diff:
```python
import functools

import jax
import jax.numpy as jnp
import numpy as np
from jax import lax
from jax.experimental import pallas as pl
from jax.experimental.pallas import tpu as pltpu
from jax.sharding import PartitionSpec as P

AXES = ("dp", "tensor")
Z_HI, Y, CORES, Z_LO, X = 4, 8, 2, 4, 4
WIDTH, D, ROWS = 896, 4096, 32
STEPS = (0, 1, -1, 2)
MIB = 1 << 20


def moves(axis, step):
    pairs = []
    for zh, y, c, zl, x in np.ndindex(Z_HI, Y, CORES, Z_LO, X):
        z = zh * Z_LO + zl
        if axis == c:
            to_z, to_x = z, (x + step) % X
        else:
            to_z, to_x = (z + step) % (Z_HI * Z_LO), x
        source = (((zh * Y + y) * CORES + c) * Z_LO + zl) * X + x
        target = (((to_z // Z_LO * Y + y) * CORES + c) * Z_LO + to_z % Z_LO) * X + to_x
        pairs.append((source, target))
    return pairs


def send(value, axis, step):
    return lax.ppermute(value, AXES, moves(axis, step))


def vmem(shape):
    return pltpu.VMEM(shape, jnp.bfloat16)


def in_vmem(*arrays):
    return [pltpu.with_memory_space_constraint(a, pltpu.VMEM) for a in arrays]


def whole():
    return pl.BlockSpec(memory_space=pltpu.VMEM)


def activate_kernel(gate_ref, up_ref, own, plus1, minus1, plus2, minus2, gate_buf, up_buf, sems):
    dp, tensor = lax.axis_index("dp"), lax.axis_index("tensor")
    core = lax.rem(dp, CORES)
    zl, x = lax.div(tensor, X), lax.rem(tensor, X)
    copies = []
    for k, first in enumerate(STEPS):
        for j, second in enumerate(STEPS):
            by_z = jnp.where(core == 0, second, first)
            by_x = jnp.where(core == 0, first, second)
            block = lax.rem(zl + by_z + Z_LO, Z_LO) * X + lax.rem(x + by_x + X, X)
            columns = pl.ds(pl.multiple_of(block * WIDTH, 128), WIDTH)
            slot = 4 * k + j
            pair = (
                pltpu.make_async_copy(gate_ref.at[:, columns], gate_buf.at[slot], sems.at[0, slot]),
                pltpu.make_async_copy(up_ref.at[:, columns], up_buf.at[slot], sems.at[1, slot]),
            )
            for copy in pair:
                copy.start()
            copies.append(pair)
    for k in range(4):
        for j in range(4):
            slot = 4 * k + j
            for copy in copies[slot]:
                copy.wait()
            gate = gate_buf[slot].astype(jnp.float32)
            hidden = (jax.nn.silu(gate) * up_buf[slot].astype(jnp.float32)).astype(jnp.bfloat16)
            if k < 3:
                (own, plus1, minus1)[k][j] = hidden
            else:
                plus2[j] = hidden[:16]
                minus2[j] = hidden[16:]


def activate(gate_pre, up_pre):
    full, half = vmem((4, 32, WIDTH)), vmem((4, 16, WIDTH))
    return pl.pallas_call(
        activate_kernel,
        out_shape=[full, full, full, half, half],
        in_specs=[pl.BlockSpec(memory_space=pl.ANY)] * 2,
        out_specs=[whole()] * 5,
        scratch_shapes=[
            pltpu.VMEM((16, ROWS, WIDTH), jnp.bfloat16),
            pltpu.VMEM((16, ROWS, WIDTH), jnp.bfloat16),
            pltpu.SemaphoreType.DMA((2, 16)),
        ],
        compiler_params=pltpu.CompilerParams(vmem_limit_bytes=8 * MIB),
        name="activate",
    )(gate_pre, up_pre)


SPANS = ((0, 32), (32, 64), (64, 96), (96, 112), (112, 128))


def pack_kernel(*refs):
    parts, outs = refs[:5], refs[5:]
    for j in range(3):
        for part, (low, high) in zip(parts, SPANS):
            outs[j][low:high, :] = part[j]
    for part, (low, high) in zip(parts, SPANS):
        if high <= 64:
            outs[3][low:high, :] = part[3]
        else:
            outs[4][low - 64 : high - 64, :] = part[3]


def pack(*parts):
    full, half = vmem((128, WIDTH)), vmem((64, WIDTH))
    return pl.pallas_call(
        pack_kernel,
        out_shape=[full, full, full, half, half],
        in_specs=[whole()] * 5,
        out_specs=[whole()] * 5,
        compiler_params=pltpu.CompilerParams(vmem_limit_bytes=4 * MIB),
        name="pack",
    )(*in_vmem(*parts))


TILE = 512


def project_kernel(count, *refs):
    rows, weight, outs, held = refs[:count], refs[count], refs[count + 1 : -1], refs[-1]
    low = 0
    for part in rows:
        held[low : low + part.shape[0], :] = part[...]
        low += part.shape[0]

    @pl.loop(0, D // TILE)
    def _(step):
        columns = pl.ds(pl.multiple_of(step * TILE, TILE), TILE)
        terms = jnp.dot(held[...], weight[:, columns], preferred_element_type=jnp.float32)
        low = 0
        for out in outs:
            out[:, columns] = terms[low : low + out.shape[0]].astype(jnp.bfloat16)
            low += out.shape[0]


def project(weight, *rows):
    total = sum(part.shape[0] for part in rows)
    return pl.pallas_call(
        functools.partial(project_kernel, len(rows)),
        out_shape=[vmem((part.shape[0], D)) for part in rows],
        in_specs=[whole()] * (len(rows) + 1),
        out_specs=[whole()] * len(rows),
        scratch_shapes=[pltpu.VMEM((total, WIDTH), jnp.bfloat16)],
        cost_estimate=pl.CostEstimate(
            flops=2 * total * WIDTH * D, bytes_accessed=2 * WIDTH * D, transcendentals=0
        ),
        compiler_params=pltpu.CompilerParams(vmem_limit_bytes=8 * MIB),
        name="project",
    )(*in_vmem(*rows, weight))


def add_kernel(spans, own, plus1, minus1, plus2, minus2, *outs):
    half = plus2.shape[0]

    @pl.loop(0, D // TILE)
    def _(step):
        columns = pl.ds(pl.multiple_of(step * TILE, TILE), TILE)
        for out, (low, high) in zip(outs, spans):
            far = plus2[low:high, columns] if high <= half else minus2[low - half : high - half, columns]
            out[:, columns] = (
                own[low:high, columns].astype(jnp.float32)
                + plus1[low:high, columns].astype(jnp.float32)
                + minus1[low:high, columns].astype(jnp.float32)
                + far.astype(jnp.float32)
            ).astype(jnp.bfloat16)


def add_up(spans, *parts):
    return pl.pallas_call(
        functools.partial(add_kernel, spans),
        out_shape=[vmem((high - low, D)) for low, high in spans],
        in_specs=[whole()] * 5,
        out_specs=[whole()] * len(spans),
        compiler_params=pltpu.CompilerParams(vmem_limit_bytes=8 * MIB),
        name="add_up",
    )(*in_vmem(*parts))


def final_kernel(own, plus1, minus1, plus2, minus2, out):
    for low, far in ((0, plus2), (16, minus2)):
        rows = slice(low, low + 16)
        out[rows, :] = (
            own[rows, :].astype(jnp.float32)
            + plus1[rows, :].astype(jnp.float32)
            + minus1[rows, :].astype(jnp.float32)
            + far[...].astype(jnp.float32)
        ).astype(jnp.bfloat16)


def final_sum(*parts):
    return pl.pallas_call(
        final_kernel,
        out_shape=jax.ShapeDtypeStruct((ROWS, D), jnp.bfloat16),
        in_specs=[whole()] * 5,
        out_specs=whole(),
        compiler_params=pltpu.CompilerParams(vmem_limit_bytes=4 * MIB),
        name="final_sum",
    )(*in_vmem(*parts))


FAR = (1, -1, 2, -2)


def shards(gate_pre, up_pre, down_weight):
    own, *away = activate(gate_pre, up_pre)
    came = [send(part, 0, step) for part, step in zip(away, FAR)]
    here, *away = pack(own, *came)
    came = [send(part, 1, step) for part, step in zip(away, FAR)]
    near = project(down_weight, came[0], came[1])
    back = [send(part, 1, -step) for part, step in zip(near, FAR[:2])]
    *far, here = project(down_weight, came[2], came[3], here)
    back += [send(part, 1, -step) for part, step in zip(far, FAR[2:])]
    here, *away = add_up(SPANS, here, *back)
    back = [send(part, 0, -step) for part, step in zip(away, FAR)]
    return final_sum(here, *back)


def solution(mesh):
    return jax.shard_map(
        shards,
        mesh=mesh,
        in_specs=(P(("dp", "tensor"), None), P(("dp", "tensor"), None), P("tensor", None)),
        out_specs=P(("dp", "tensor"), None),
        check_vma=False,
    )
```

time: 165 us -> 125 us (0.76)
  the two profiles are of different devices: /device:TPU:56 before, /device:TPU:66 now
where the time goes in v1:
time: 125 us; the launch traced here: 124 us
  starting transfers between devices  66.9 us (54%)
  waiting for transfers between devices  41.6 us (33%)
  Pallas kernels  10.1 us (8%)
  local copies, waits for them, and re-layouts  5.47 us (4%)
    ppermute x16, starting transfers between devices, send(): return lax.ppermute(value, AXES, moves(axis, step))  66.9 us
    ppermute x16, waiting for transfers between devices, send(): return lax.ppermute(value, AXES, moves(axis, step))  41.6 us
    pallas_call x2, Pallas kernels, project(): pl.pallas_call(functools.partial(project_kernel, len(rows)), out_shape=[v...  7.17 us
    unnamed x8, local copies, waits for them, and re-layouts  5.47 us
  transfers between devices with their start and end apart: 16, of which 8 were waited for; matrix products, arithmetic and copies ran while one was open for 0% of the time, Pallas kernels for 3%

profile of v1, /device:TPU:66, one launch (start us, length us, event | category | flops | bytes accessed | tf_op | source)
XLA Modules:
  0.0 124.3 jit_solution(9670521844396729046)
XLA Ops:
  0.0 0.0 copy-start.2
  0.0 1.2 copy-done.2
  1.2 0.0 copy-start.3
  1.2 1.2 copy-done.3
  2.4 1.5 %activate.1 = (bf16[4,32,896]{2,1,0:T(8,128)(2,1)S(1)}, bf16[4,32,896]{2,1,0:T(8,128)(2,1)S(1)}, bf16[4,32,896]{2,1,0:T(8,128)(2,1)S(1)}, bf16[4,16,896]{2,1,0:T(8,128)(2,1)S(1)}, bf16[4,16,896]{2,1,0:T(8,128)(2,1)S(1)}) custom-call(bf16[32,14336]{1,0:T(8,128)(2,1)S(1)} %copy-done.2, bf16[32,14336]{1,0:T(8,128)(2,1)S(1)} %copy-done.3), custom_call_target="tpu_custom_call" | custom-call | tf_op jit(solution)/shard_map/activate/pallas_call | solution.py:83
  3.8 3.4 %collective-permute-start = (bf16[4,32,896]{2,1,0:T(8,128)(2,1)S(1)}, bf16[4,32,896]{2,1,0:T(8,128)(2,1)S(1)}, u32[]{:S(2)}, u32[]{:S(2)}) collective-permute-start(bf16[4,32,896]{2,1,0:T(8,128)(2,1)S(1)} %get-tuple-element.26), channel_id=1, source_target_pairs={{0,1},{1,2},{2,3},{3,0},{4,5},{5,6},{6,7},{7,4},{8,9},{9,10},{10,1... | collective-permute-start | bytes 688136 | tf_op jit(solution)/shard_map/ppermute | solution.py:33
  7.2 2.4 %collective-permute-start.1 = (bf16[4,32,896]{2,1,0:T(8,128)(2,1)S(1)}, bf16[4,32,896]{2,1,0:T(8,128)(2,1)S(1)}, u32[]{:S(2)}, u32[]{:S(2)}) collective-permute-start(bf16[4,32,896]{2,1,0:T(8,128)(2,1)S(1)} %get-tuple-element.27), channel_id=1, source_target_pairs={{0,3},{1,0},{2,1},{3,2},{4,7},{5,4},{6,5},{7,6},{8,11},{9,8},{10,9... | collective-permute-start | bytes 688136 | tf_op jit(solution)/shard_map/ppermute | solution.py:33
  9.7 4.0 %collective-permute-start.2 = (bf16[4,16,896]{2,1,0:T(8,128)(2,1)S(1)}, bf16[4,16,896]{2,1,0:T(8,128)(2,1)S(1)}, u32[]{:S(2)}, u32[]{:S(2)}) collective-permute-start(bf16[4,16,896]{2,1,0:T(8,128)(2,1)S(1)} %get-tuple-element.28), channel_id=1, source_target_pairs={{0,2},{1,3},{2,0},{3,1},{4,6},{5,7},{6,4},{7,5},{8,10},{9,11},{10,... | collective-permute-start | bytes 344072 | tf_op jit(solution)/shard_map/ppermute | solution.py:33
  13.7 3.3 %collective-permute-start.3 = (bf16[4,16,896]{2,1,0:T(8,128)(2,1)S(1)}, bf16[4,16,896]{2,1,0:T(8,128)(2,1)S(1)}, u32[]{:S(2)}, u32[]{:S(2)}) collective-permute-start(bf16[4,16,896]{2,1,0:T(8,128)(2,1)S(1)} %get-tuple-element.29), channel_id=1, source_target_pairs={{0,2},{1,3},{2,0},{3,1},{4,6},{5,7},{6,4},{7,5},{8,10},{9,11},{10,... | collective-permute-start | bytes 344072 | tf_op jit(solution)/shard_map/ppermute | solution.py:33
  17.1 0.8 collective-permute-done.2.refs_3_
  17.9 4.0 %collective-permute-done.3.refs_4_ = bf16[4,16,896]{2,1,0:T(8,128)(2,1)S(1)} collective-permute-done((bf16[4,16,896]{2,1,0:T(8,128)(2,1)S(1)}, bf16[4,16,896]{2,1,0:T(8,128)(2,1)S(1)}, u32[]{:S(2)}, u32[]{:S(2)}) %collective-permute-start.3) | collective-permute-done | bytes 114720 | tf_op jit(solution)/shard_map/ppermute | solution.py:33
  21.9 0.0 collective-permute-done.refs_1_
  21.9 0.0 collective-permute-done.1.refs_2_
  21.9 0.1 pack.1
  22.0 4.3 %collective-permute-start.6 = (bf16[128,896]{1,0:T(8,128)(2,1)S(1)}, bf16[128,896]{1,0:T(8,128)(2,1)S(1)}, u32[]{:S(2)}, u32[]{:S(2)}) collective-permute-start(bf16[128,896]{1,0:T(8,128)(2,1)S(1)} %get-tuple-element.34), channel_id=1, source_target_pairs={{0,4},{1,5},{2,6},{3,7},{4,8},{5,9},{6,10},{7,11},{8,12},{9,13},{1... | collective-permute-start | bytes 688136 | tf_op jit(solution)/shard_map/ppermute | solution.py:33
  26.3 10.3 %collective-permute-start.7 = (bf16[128,896]{1,0:T(8,128)(2,1)S(1)}, bf16[128,896]{1,0:T(8,128)(2,1)S(1)}, u32[]{:S(2)}, u32[]{:S(2)}) collective-permute-start(bf16[128,896]{1,0:T(8,128)(2,1)S(1)} %get-tuple-element.35), channel_id=1, source_target_pairs={{0,780},{1,781},{2,782},{3,783},{4,0},{5,1},{6,2},{7,3},{8,4},{9,5... | collective-permute-start | bytes 688136 | tf_op jit(solution)/shard_map/ppermute | solution.py:33
  36.6 2.1 %collective-permute-done.6.refs_0_ = bf16[128,896]{1,0:T(8,128)(2,1)S(1)} collective-permute-done((bf16[128,896]{1,0:T(8,128)(2,1)S(1)}, bf16[128,896]{1,0:T(8,128)(2,1)S(1)}, u32[]{:S(2)}, u32[]{:S(2)}) %collective-permute-start.6) | collective-permute-done | bytes 229408 | tf_op jit(solution)/shard_map/ppermute | solution.py:33
  38.7 1.5 %collective-permute-done.7.refs_1_ = bf16[128,896]{1,0:T(8,128)(2,1)S(1)} collective-permute-done((bf16[128,896]{1,0:T(8,128)(2,1)S(1)}, bf16[128,896]{1,0:T(8,128)(2,1)S(1)}, u32[]{:S(2)}, u32[]{:S(2)}) %collective-permute-start.7) | collective-permute-done | bytes 229408 | tf_op jit(solution)/shard_map/ppermute | solution.py:33
  40.1 0.0 copy-start
  40.1 3.1 %copy-done = bf16[896,4096]{1,0:T(8,128)(2,1)S(1)} copy-done((bf16[896,4096]{1,0:T(8,128)(2,1)S(1)}, bf16[896,4096]{1,0:T(8,128)(2,1)}, u32[]{:S(2)}) %copy-start) | copy-done | bytes 7340056
  43.2 0.0 copy-start.1
  43.2 3.6 %project.3 = (bf16[128,4096]{1,0:T(8,128)(2,1)S(1)}, bf16[128,4096]{1,0:T(8,128)(2,1)S(1)}) custom-call(bf16[128,896]{1,0:T(8,128)(2,1)S(1)} %collective-permute-done.6.refs_0_, bf16[128,896]{1,0:T(8,128)(2,1)S(1)} %collective-permute-done.7.refs_1_, bf16[896,4096]{1,0:T(8,128)(2,1)S(1)} %copy-done), custom_call_target="tpu_custom_call" | custom-call | flops 1879048192 | bytes 7340032 | tf_op jit(solution)/shard_map/project/pallas_call | solution.py:147
  46.8 7.1 %collective-permute-start.8 = (bf16[128,4096]{1,0:T(8,128)(2,1)S(1)}, bf16[128,4096]{1,0:T(8,128)(2,1)S(1)}, u32[]{:S(2)}, u32[]{:S(2)}) collective-permute-start(bf16[128,4096]{1,0:T(8,128)(2,1)S(1)} %get-tuple-element.36), channel_id=1, source_target_pairs={{0,780},{1,781},{2,782},{3,783},{4,0},{5,1},{6,2},{7,3},{8,4},{9,5... | collective-permute-start | bytes 3145736 | tf_op jit(solution)/shard_map/ppermute | solution.py:33
  54.0 1.9 %collective-permute-start.9 = (bf16[128,4096]{1,0:T(8,128)(2,1)S(1)}, bf16[128,4096]{1,0:T(8,128)(2,1)S(1)}, u32[]{:S(2)}, u32[]{:S(2)}) collective-permute-start(bf16[128,4096]{1,0:T(8,128)(2,1)S(1)} %get-tuple-element.37), channel_id=1, source_target_pairs={{0,4},{1,5},{2,6},{3,7},{4,8},{5,9},{6,10},{7,11},{8,12},{9,13},{1... | collective-permute-start | bytes 3145736 | tf_op jit(solution)/shard_map/ppermute | solution.py:33
  55.9 1.9 %collective-permute-start.4 = (bf16[64,896]{1,0:T(8,128)(2,1)S(1)}, bf16[64,896]{1,0:T(8,128)(2,1)S(1)}, u32[]{:S(2)}, u32[]{:S(2)}) collective-permute-start(bf16[64,896]{1,0:T(8,128)(2,1)S(1)} %get-tuple-element.30), channel_id=1, source_target_pairs={{0,8},{1,9},{2,10},{3,11},{4,12},{5,13},{6,14},{7,15},{8,256},{9,2... | collective-permute-start | bytes 344072 | tf_op jit(solution)/shard_map/ppermute | solution.py:33
  57.8 8.3 %collective-permute-start.5 = (bf16[64,896]{1,0:T(8,128)(2,1)S(1)}, bf16[64,896]{1,0:T(8,128)(2,1)S(1)}, u32[]{:S(2)}, u32[]{:S(2)}) collective-permute-start(bf16[64,896]{1,0:T(8,128)(2,1)S(1)} %get-tuple-element.31), channel_id=1, source_target_pairs={{0,776},{1,777},{2,778},{3,779},{4,780},{5,781},{6,782},{7,783},{8... | collective-permute-start | bytes 344072 | tf_op jit(solution)/shard_map/ppermute | solution.py:33
  66.1 11.4 %collective-permute-done.4.refs_0_ = bf16[64,896]{1,0:T(8,128)(2,1)S(1)} collective-permute-done((bf16[64,896]{1,0:T(8,128)(2,1)S(1)}, bf16[64,896]{1,0:T(8,128)(2,1)S(1)}, u32[]{:S(2)}, u32[]{:S(2)}) %collective-permute-start.4) | collective-permute-done | bytes 114720 | tf_op jit(solution)/shard_map/ppermute | solution.py:33
  77.4 0.0 collective-permute-done.5.refs_1_
  77.5 0.0 copy-done.1
  77.5 3.6 %project.2 = (bf16[64,4096]{1,0:T(8,128)(2,1)S(1)}, bf16[64,4096]{1,0:T(8,128)(2,1)S(1)}, bf16[128,4096]{1,0:T(8,128)(2,1)S(1)}) custom-call(bf16[64,896]{1,0:T(8,128)(2,1)S(1)} %collective-permute-done.4.refs_0_, bf16[64,896]{1,0:T(8,128)(2,1)S(1)} %collective-permute-done.5.refs_1_, bf16[128,896]{1,0:T(8,128)(2,1)S(1)} %get-tuple-element.32.refs_2_, ...), custom_call_target="tpu_custom_call" | custom-call | flops 1879048192 | bytes 7340032 | tf_op jit(solution)/shard_map/project/pallas_call | solution.py:147
  81.0 1.9 %collective-permute-start.10 = (bf16[64,4096]{1,0:T(8,128)(2,1)S(1)}, bf16[64,4096]{1,0:T(8,128)(2,1)S(1)}, u32[]{:S(2)}, u32[]{:S(2)}) collective-permute-start(bf16[64,4096]{1,0:T(8,128)(2,1)S(1)} %get-tuple-element.38), channel_id=1, source_target_pairs={{0,776},{1,777},{2,778},{3,779},{4,780},{5,781},{6,782},{7,783},{8... | collective-permute-start | bytes 1572872 | tf_op jit(solution)/shard_map/ppermute | solution.py:33
  83.0 4.8 %collective-permute-start.11 = (bf16[64,4096]{1,0:T(8,128)(2,1)S(1)}, bf16[64,4096]{1,0:T(8,128)(2,1)S(1)}, u32[]{:S(2)}, u32[]{:S(2)}) collective-permute-start(bf16[64,4096]{1,0:T(8,128)(2,1)S(1)} %get-tuple-element.39), channel_id=1, source_target_pairs={{0,8},{1,9},{2,10},{3,11},{4,12},{5,13},{6,14},{7,15},{8,256},{9,2... | collective-permute-start | bytes 1572872 | tf_op jit(solution)/shard_map/ppermute | solution.py:33
  87.8 16.3 %collective-permute-done.10.plus2 = bf16[64,4096]{1,0:T(8,128)(2,1)S(1)} collective-permute-done((bf16[64,4096]{1,0:T(8,128)(2,1)S(1)}, bf16[64,4096]{1,0:T(8,128)(2,1)S(1)}, u32[]{:S(2)}, u32[]{:S(2)}) %collective-permute-start.10) | collective-permute-done | bytes 524320 | tf_op jit(solution)/shard_map/ppermute | solution.py:33
  104.1 0.0 collective-permute-done.11.minus2
  104.1 0.0 collective-permute-done.8.plus1
  104.1 0.0 collective-permute-done.9.minus1
  104.1 0.6 add_up.1
  104.7 1.9 %collective-permute-start.12 = (bf16[32,4096]{1,0:T(8,128)(2,1)S(1)}, bf16[32,4096]{1,0:T(8,128)(2,1)S(1)}, u32[]{:S(2)}, u32[]{:S(2)}) collective-permute-start(bf16[32,4096]{1,0:T(8,128)(2,1)S(1)} %get-tuple-element.41), channel_id=1, source_target_pairs={{0,3},{1,0},{2,1},{3,2},{4,7},{5,4},{6,5},{7,6},{8,11},{9,8},{10,9... | collective-permute-start | bytes 786440 | tf_op jit(solution)/shard_map/ppermute | solution.py:33
  106.6 3.9 %collective-permute-start.13 = (bf16[32,4096]{1,0:T(8,128)(2,1)S(1)}, bf16[32,4096]{1,0:T(8,128)(2,1)S(1)}, u32[]{:S(2)}, u32[]{:S(2)}) collective-permute-start(bf16[32,4096]{1,0:T(8,128)(2,1)S(1)} %get-tuple-element.42), channel_id=1, source_target_pairs={{0,1},{1,2},{2,3},{3,0},{4,5},{5,6},{6,7},{7,4},{8,9},{9,10},{10,1... | collective-permute-start | bytes 786440 | tf_op jit(solution)/shard_map/ppermute | solution.py:33
  110.6 4.5 %collective-permute-start.14 = (bf16[16,4096]{1,0:T(8,128)(2,1)S(1)}, bf16[16,4096]{1,0:T(8,128)(2,1)S(1)}, u32[]{:S(2)}, u32[]{:S(2)}) collective-permute-start(bf16[16,4096]{1,0:T(8,128)(2,1)S(1)} %get-tuple-element.43), channel_id=1, source_target_pairs={{0,2},{1,3},{2,0},{3,1},{4,6},{5,7},{6,4},{7,5},{8,10},{9,11},{10,... | collective-permute-start | bytes 393224 | tf_op jit(solution)/shard_map/ppermute | solution.py:33
  115.1 2.8 %collective-permute-start.15 = (bf16[16,4096]{1,0:T(8,128)(2,1)S(1)}, bf16[16,4096]{1,0:T(8,128)(2,1)S(1)}, u32[]{:S(2)}, u32[]{:S(2)}) collective-permute-start(bf16[16,4096]{1,0:T(8,128)(2,1)S(1)} %get-tuple-element.44), channel_id=1, source_target_pairs={{0,2},{1,3},{2,0},{3,1},{4,6},{5,7},{6,4},{7,5},{8,10},{9,11},{10,... | collective-permute-start | bytes 393224 | tf_op jit(solution)/shard_map/ppermute | solution.py:33
  117.9 1.0 collective-permute-done.14.plus2
  118.9 4.6 %collective-permute-done.15.minus2 = bf16[16,4096]{1,0:T(8,128)(2,1)S(1)} collective-permute-done((bf16[16,4096]{1,0:T(8,128)(2,1)S(1)}, bf16[16,4096]{1,0:T(8,128)(2,1)S(1)}, u32[]{:S(2)}, u32[]{:S(2)}) %collective-permute-start.15) | collective-permute-done | bytes 131104 | tf_op jit(solution)/shard_map/ppermute | solution.py:33
  123.5 0.0 collective-permute-done.12.plus1
  123.5 0.0 collective-permute-done.13.minus1
  123.5 0.8 final_sum.1
Async XLA Ops:
  0.0 1.2 copy-start.2
  1.2 1.2 copy-start.3
  3.8 18.1 %collective-permute-start = (bf16[4,32,896]{2,1,0:T(8,128)(2,1)S(1)}, bf16[4,32,896]{2,1,0:T(8,128)(2,1)S(1)}, u32[]{:S(2)}, u32[]{:S(2)}) collective-permute-start(bf16[4,32,896]{2,1,0:T(8,128)(2,1)S(1)} %get-tuple-element.26), channel_id=1, source_target_pairs={{0,1},{1,2},{2,3},{3,0},{4,5},{5,6},{6,7},{7,4},{8,9},{9,10},{10,1... | collective-permute-start | bytes 688136 | tf_op jit(solution)/shard_map/ppermute | solution.py:33
  7.2 14.7 %collective-permute-start.1 = (bf16[4,32,896]{2,1,0:T(8,128)(2,1)S(1)}, bf16[4,32,896]{2,1,0:T(8,128)(2,1)S(1)}, u32[]{:S(2)}, u32[]{:S(2)}) collective-permute-start(bf16[4,32,896]{2,1,0:T(8,128)(2,1)S(1)} %get-tuple-element.27), channel_id=1, source_target_pairs={{0,3},{1,0},{2,1},{3,2},{4,7},{5,4},{6,5},{7,6},{8,11},{9,8},{10,9... | collective-permute-start | bytes 688136 | tf_op jit(solution)/shard_map/ppermute | solution.py:33
  9.7 8.2 %collective-permute-start.2 = (bf16[4,16,896]{2,1,0:T(8,128)(2,1)S(1)}, bf16[4,16,896]{2,1,0:T(8,128)(2,1)S(1)}, u32[]{:S(2)}, u32[]{:S(2)}) collective-permute-start(bf16[4,16,896]{2,1,0:T(8,128)(2,1)S(1)} %get-tuple-element.28), channel_id=1, source_target_pairs={{0,2},{1,3},{2,0},{3,1},{4,6},{5,7},{6,4},{7,5},{8,10},{9,11},{10,... | collective-permute-start | bytes 344072 | tf_op jit(solution)/shard_map/ppermute | solution.py:33
  13.7 8.2 %collective-permute-start.3 = (bf16[4,16,896]{2,1,0:T(8,128)(2,1)S(1)}, bf16[4,16,896]{2,1,0:T(8,128)(2,1)S(1)}, u32[]{:S(2)}, u32[]{:S(2)}) collective-permute-start(bf16[4,16,896]{2,1,0:T(8,128)(2,1)S(1)} %get-tuple-element.29), channel_id=1, source_target_pairs={{0,2},{1,3},{2,0},{3,1},{4,6},{5,7},{6,4},{7,5},{8,10},{9,11},{10,... | collective-permute-start | bytes 344072 | tf_op jit(solution)/shard_map/ppermute | solution.py:33
  22.0 16.7 %collective-permute-start.6 = (bf16[128,896]{1,0:T(8,128)(2,1)S(1)}, bf16[128,896]{1,0:T(8,128)(2,1)S(1)}, u32[]{:S(2)}, u32[]{:S(2)}) collective-permute-start(bf16[128,896]{1,0:T(8,128)(2,1)S(1)} %get-tuple-element.34), channel_id=1, source_target_pairs={{0,4},{1,5},{2,6},{3,7},{4,8},{5,9},{6,10},{7,11},{8,12},{9,13},{1... | collective-permute-start | bytes 688136 | tf_op jit(solution)/shard_map/ppermute | solution.py:33
  26.3 13.8 %collective-permute-start.7 = (bf16[128,896]{1,0:T(8,128)(2,1)S(1)}, bf16[128,896]{1,0:T(8,128)(2,1)S(1)}, u32[]{:S(2)}, u32[]{:S(2)}) collective-permute-start(bf16[128,896]{1,0:T(8,128)(2,1)S(1)} %get-tuple-element.35), channel_id=1, source_target_pairs={{0,780},{1,781},{2,782},{3,783},{4,0},{5,1},{6,2},{7,3},{8,4},{9,5... | collective-permute-start | bytes 688136 | tf_op jit(solution)/shard_map/ppermute | solution.py:33
  40.1 3.1 %copy-start = (bf16[896,4096]{1,0:T(8,128)(2,1)S(1)}, bf16[896,4096]{1,0:T(8,128)(2,1)}, u32[]{:S(2)}) copy-start(bf16[896,4096]{1,0:T(8,128)(2,1)} %refs_2_.1) | copy-start | bytes 22020100
  43.2 34.2 %copy-start.1 = (bf16[896,4096]{1,0:T(8,128)(2,1)S(1)}, bf16[896,4096]{1,0:T(8,128)(2,1)}, u32[]{:S(2)}) copy-start(bf16[896,4096]{1,0:T(8,128)(2,1)} %refs_2_.1) | copy-start | bytes 22020100
  46.8 57.3 %collective-permute-start.8 = (bf16[128,4096]{1,0:T(8,128)(2,1)S(1)}, bf16[128,4096]{1,0:T(8,128)(2,1)S(1)}, u32[]{:S(2)}, u32[]{:S(2)}) collective-permute-start(bf16[128,4096]{1,0:T(8,128)(2,1)S(1)} %get-tuple-element.36), channel_id=1, source_target_pairs={{0,780},{1,781},{2,782},{3,783},{4,0},{5,1},{6,2},{7,3},{8,4},{9,5... | collective-permute-start | bytes 3145736 | tf_op jit(solution)/shard_map/ppermute | solution.py:33
  54.0 50.2 %collective-permute-start.9 = (bf16[128,4096]{1,0:T(8,128)(2,1)S(1)}, bf16[128,4096]{1,0:T(8,128)(2,1)S(1)}, u32[]{:S(2)}, u32[]{:S(2)}) collective-permute-start(bf16[128,4096]{1,0:T(8,128)(2,1)S(1)} %get-tuple-element.37), channel_id=1, source_target_pairs={{0,4},{1,5},{2,6},{3,7},{4,8},{5,9},{6,10},{7,11},{8,12},{9,13},{1... | collective-permute-start | bytes 3145736 | tf_op jit(solution)/shard_map/ppermute | solution.py:33
  55.9 21.6 %collective-permute-start.4 = (bf16[64,896]{1,0:T(8,128)(2,1)S(1)}, bf16[64,896]{1,0:T(8,128)(2,1)S(1)}, u32[]{:S(2)}, u32[]{:S(2)}) collective-permute-start(bf16[64,896]{1,0:T(8,128)(2,1)S(1)} %get-tuple-element.30), channel_id=1, source_target_pairs={{0,8},{1,9},{2,10},{3,11},{4,12},{5,13},{6,14},{7,15},{8,256},{9,2... | collective-permute-start | bytes 344072 | tf_op jit(solution)/shard_map/ppermute | solution.py:33
  57.8 19.6 %collective-permute-start.5 = (bf16[64,896]{1,0:T(8,128)(2,1)S(1)}, bf16[64,896]{1,0:T(8,128)(2,1)S(1)}, u32[]{:S(2)}, u32[]{:S(2)}) collective-permute-start(bf16[64,896]{1,0:T(8,128)(2,1)S(1)} %get-tuple-element.31), channel_id=1, source_target_pairs={{0,776},{1,777},{2,778},{3,779},{4,780},{5,781},{6,782},{7,783},{8... | collective-permute-start | bytes 344072 | tf_op jit(solution)/shard_map/ppermute | solution.py:33
  81.0 23.1 %collective-permute-start.10 = (bf16[64,4096]{1,0:T(8,128)(2,1)S(1)}, bf16[64,4096]{1,0:T(8,128)(2,1)S(1)}, u32[]{:S(2)}, u32[]{:S(2)}) collective-permute-start(bf16[64,4096]{1,0:T(8,128)(2,1)S(1)} %get-tuple-element.38), channel_id=1, source_target_pairs={{0,776},{1,777},{2,778},{3,779},{4,780},{5,781},{6,782},{7,783},{8... | collective-permute-start | bytes 1572872 | tf_op jit(solution)/shard_map/ppermute | solution.py:33
  83.0 21.2 %collective-permute-start.11 = (bf16[64,4096]{1,0:T(8,128)(2,1)S(1)}, bf16[64,4096]{1,0:T(8,128)(2,1)S(1)}, u32[]{:S(2)}, u32[]{:S(2)}) collective-permute-start(bf16[64,4096]{1,0:T(8,128)(2,1)S(1)} %get-tuple-element.39), channel_id=1, source_target_pairs={{0,8},{1,9},{2,10},{3,11},{4,12},{5,13},{6,14},{7,15},{8,256},{9,2... | collective-permute-start | bytes 1572872 | tf_op jit(solution)/shard_map/ppermute | solution.py:33
  104.7 18.8 %collective-permute-start.12 = (bf16[32,4096]{1,0:T(8,128)(2,1)S(1)}, bf16[32,4096]{1,0:T(8,128)(2,1)S(1)}, u32[]{:S(2)}, u32[]{:S(2)}) collective-permute-start(bf16[32,4096]{1,0:T(8,128)(2,1)S(1)} %get-tuple-element.41), channel_id=1, source_target_pairs={{0,3},{1,0},{2,1},{3,2},{4,7},{5,4},{6,5},{7,6},{8,11},{9,8},{10,9... | collective-permute-start | bytes 786440 | tf_op jit(solution)/shard_map/ppermute | solution.py:33
  106.6 16.9 %collective-permute-start.13 = (bf16[32,4096]{1,0:T(8,128)(2,1)S(1)}, bf16[32,4096]{1,0:T(8,128)(2,1)S(1)}, u32[]{:S(2)}, u32[]{:S(2)}) collective-permute-start(bf16[32,4096]{1,0:T(8,128)(2,1)S(1)} %get-tuple-element.42), channel_id=1, source_target_pairs={{0,1},{1,2},{2,3},{3,0},{4,5},{5,6},{6,7},{7,4},{8,9},{9,10},{10,1... | collective-permute-start | bytes 786440 | tf_op jit(solution)/shard_map/ppermute | solution.py:33
  110.6 8.4 %collective-permute-start.14 = (bf16[16,4096]{1,0:T(8,128)(2,1)S(1)}, bf16[16,4096]{1,0:T(8,128)(2,1)S(1)}, u32[]{:S(2)}, u32[]{:S(2)}) collective-permute-start(bf16[16,4096]{1,0:T(8,128)(2,1)S(1)} %get-tuple-element.43), channel_id=1, source_target_pairs={{0,2},{1,3},{2,0},{3,1},{4,6},{5,7},{6,4},{7,5},{8,10},{9,11},{10,... | collective-permute-start | bytes 393224 | tf_op jit(solution)/shard_map/ppermute | solution.py:33
  115.1 8.4 %collective-permute-start.15 = (bf16[16,4096]{1,0:T(8,128)(2,1)S(1)}, bf16[16,4096]{1,0:T(8,128)(2,1)S(1)}, u32[]{:S(2)}, u32[]{:S(2)}) collective-permute-start(bf16[16,4096]{1,0:T(8,128)(2,1)S(1)} %get-tuple-element.44), channel_id=1, source_target_pairs={{0,2},{1,3},{2,0},{3,1},{4,6},{5,7},{6,4},{7,5},{8,10},{9,11},{10,... | collective-permute-start | bytes 393224 | tf_op jit(solution)/shard_map/ppermute | solution.py:33

commit v2 on v0

v2 whole, which is shorter than its diff:
```python
import jax
import jax.numpy as jnp
import numpy as np
from jax import lax
from jax.experimental import pallas as pl
from jax.experimental.pallas import tpu as pltpu
from jax.sharding import PartitionSpec as P

AXES = ("dp", "tensor")
Z_HI, Y, CORES, Z_LO, X = 4, 8, 2, 4, 4
Z = Z_HI * Z_LO
WIDTH, D, ROWS = 896, 4096, 32
BITS = ((0, 0), (0, 1), (1, 0), (1, 1))
MIB = 1 << 20


def pair_base(value, shift):
    return (value + shift) // 2 * 2 - shift


def squares(outer):
    groups = []
    for zh, y, c, zl, x in np.ndindex(Z_HI, Y, CORES, Z_LO, X):
        z, shift = zh * Z_LO + zl, c ^ outer
        z0, x0 = pair_base(z, shift), pair_base(x, shift)
        if (z0, x0) != (z, x) and (z0 % Z, x0 % X) != (z, x):
            continue
        group = []
        for bz, bx in BITS:
            to_z, to_x = (z0 + bz) % Z, (x0 + bx) % X
            group.append((((to_z // Z_LO * Y + y) * CORES + c) * Z_LO + to_z % Z_LO) * X + to_x)
        groups.append(group)
    return groups


def swap(value, outer):
    return lax.all_to_all(
        value, AXES, split_axis=0, concat_axis=0, axis_index_groups=squares(outer), tiled=True
    )


def vmem(shape):
    return pltpu.VMEM(shape, jnp.bfloat16)


def in_vmem(array):
    return pltpu.with_memory_space_constraint(array, pltpu.VMEM)


def in_hbm(array):
    return pltpu.with_memory_space_constraint(array, pltpu.HBM)


def whole():
    return pl.BlockSpec(memory_space=pltpu.VMEM)


def stays():
    return pl.BlockSpec(memory_space=pltpu.HBM)


def activate_kernel(gate_ref, up_ref, out, gate_buf, up_buf, sems):
    dp, tensor = lax.axis_index("dp"), lax.axis_index("tensor")
    core = lax.rem(dp, CORES)
    zl, x = lax.div(tensor, X), lax.rem(tensor, X)

    def member(value, shift, bit):
        return lax.div(value + shift, 2) * 2 - shift + bit

    copies = []
    for i, (oz, ox) in enumerate(BITS):
        for j, (iz, ix) in enumerate(BITS):
            to_z = member(member(zl + 4, 1 - core, oz), core, iz)
            to_x = member(member(x + 4, 1 - core, ox), core, ix)
            block = lax.rem(to_z, Z_LO) * X + lax.rem(to_x, X)
            columns = pl.ds(pl.multiple_of(block * WIDTH, 128), WIDTH)
            pair = (
                pltpu.make_async_copy(gate_ref.at[:, columns], gate_buf.at[i, j], sems.at[0, i, j]),
                pltpu.make_async_copy(up_ref.at[:, columns], up_buf.at[i, j], sems.at[1, i, j]),
            )
            for copy in pair:
                copy.start()
            copies.append(pair)
    for i in range(4):
        for j in range(4):
            for copy in copies[4 * i + j]:
                copy.wait()
            gate = gate_buf[i, j].astype(jnp.float32)
            out[i, j] = (jax.nn.silu(gate) * up_buf[i, j].astype(jnp.float32)).astype(jnp.bfloat16)


def activate(gate_pre, up_pre):
    shape = (4, 4, ROWS, WIDTH)
    return pl.pallas_call(
        activate_kernel,
        out_shape=vmem(shape),
        in_specs=[stays()] * 2,
        out_specs=whole(),
        scratch_shapes=[
            pltpu.VMEM(shape, jnp.bfloat16),
            pltpu.VMEM(shape, jnp.bfloat16),
            pltpu.SemaphoreType.DMA((2, 4, 4)),
        ],
        compiler_params=pltpu.CompilerParams(vmem_limit_bytes=8 * MIB),
        name="activate",
    )(in_hbm(gate_pre), in_hbm(up_pre))


def regroup_kernel(came, out):
    for i in range(4):
        for j in range(4):
            out[j, ROWS * i : ROWS * (i + 1), :] = came[i, j]


def regroup(came):
    return pl.pallas_call(
        regroup_kernel,
        out_shape=vmem((4, 4 * ROWS, WIDTH)),
        in_specs=[whole()],
        out_specs=whole(),
        compiler_params=pltpu.CompilerParams(vmem_limit_bytes=4 * MIB),
        name="regroup",
    )(in_vmem(came))


TILE = 512
TILES = D // TILE


def project_kernel(hidden, weight, out, held, sems):
    copies = [
        pltpu.make_async_copy(
            weight.at[:, TILE * tile : TILE * (tile + 1)], held.at[tile], sems.at[tile]
        )
        for tile in range(TILES)
    ]
    for copy in copies:
        copy.start()
    rows = hidden[...].reshape(16 * ROWS, WIDTH)
    for tile, copy in enumerate(copies):
        copy.wait()
        terms = jnp.dot(rows, held[tile], preferred_element_type=jnp.float32)
        out[:, :, TILE * tile : TILE * (tile + 1)] = terms.astype(jnp.bfloat16).reshape(4, 4 * ROWS, TILE)


def project(hidden, weight):
    return pl.pallas_call(
        project_kernel,
        out_shape=vmem((4, 4 * ROWS, D)),
        in_specs=[whole(), stays()],
        out_specs=whole(),
        scratch_shapes=[
            pltpu.VMEM((TILES, WIDTH, TILE), jnp.bfloat16),
            pltpu.SemaphoreType.DMA((TILES,)),
        ],
        cost_estimate=pl.CostEstimate(
            flops=2 * 16 * ROWS * WIDTH * D, bytes_accessed=2 * WIDTH * D, transcendentals=0
        ),
        compiler_params=pltpu.CompilerParams(vmem_limit_bytes=16 * MIB),
        name="project",
    )(in_vmem(hidden), in_hbm(weight))


def add_kernel(parts, out):
    @pl.loop(0, TILES)
    def _(tile):
        columns = pl.ds(pl.multiple_of(tile * TILE, TILE), TILE)
        total = parts[0, :, columns].astype(jnp.float32)
        for member in range(1, 4):
            total += parts[member, :, columns].astype(jnp.float32)
        out[:, columns] = total.astype(jnp.bfloat16)


def add_up(parts, out_shape):
    return pl.pallas_call(
        add_kernel,
        out_shape=out_shape,
        in_specs=[whole()],
        out_specs=whole(),
        compiler_params=pltpu.CompilerParams(vmem_limit_bytes=4 * MIB),
        name="add_up",
    )(in_vmem(parts))


def shards(gate_pre, up_pre, down_weight):
    hidden = regroup(swap(activate(gate_pre, up_pre), 1))
    terms = project(swap(hidden, 0), down_weight)
    sums = add_up(swap(terms, 0), vmem((4 * ROWS, D)))
    sums = swap(sums.reshape(4, ROWS, D), 1)
    return add_up(sums, jax.ShapeDtypeStruct((ROWS, D), jnp.bfloat16))


def solution(mesh):
    return jax.shard_map(
        shards,
        mesh=mesh,
        in_specs=(P(("dp", "tensor"), None), P(("dp", "tensor"), None), P("tensor", None)),
        out_specs=P(("dp", "tensor"), None),
        check_vma=False,
    )
```

time: 165 us -> 94.1 us (0.57)
  waiting for transfers between devices: 106 us -> 0 us
  blocking collectives: 33.8 us -> 83.5 us
  between operations: 13.4 us -> 0.03 us
  Pallas kernels: 0 us -> 10.2 us
  matrix products: 9.21 us -> 0 us
  other arithmetic: 1.97 us -> 0 us
    reduce_scatter x1 -> x0, waiting for transfers between devices: 106 us -> none  [shards(): lax.psum_scatter(terms.astype(jnp.bfloat16), 'tensor', scatter_dimension=...]
    all_to_all x1 -> x4, blocking collectives: 33.8 us -> 83.5 us  [swap(): lax.all_to_all(value, AXES, split_axis=0, concat_axis=0, axis_index_group...]
    pallas_call x0 -> x5, Pallas kernels: none -> 10.2 us  [the longest x1 6.93 us: project(): pl.pallas_call(project_kernel, out_shape=vmem((4, 4 * ROWS, D)), in_specs...]
    dot_general x1 -> x0, matrix products: 9.21 us -> none  [shards(): terms = jnp.dot(hidden, down_weight, preferred_element_type=jnp.float32)]
    convert_element_type x1 -> x0, other arithmetic: 1.97 us -> none  [activate(): (jax.nn.silu(gate_vals.astype(jnp.float32)) * up_vals.astype(jnp.float32)...]
  transfers between devices with their start and end apart: 1 -> 0, of which waited for: 1 -> 0; matrix products, arithmetic and copies ran while one was open for 0% -> 0% of each run, Pallas kernels for 0% -> 0%
where the time goes in v2:
time: 94.1 us; the launch traced here: 93.7 us
  blocking collectives  83.5 us (89%)
  Pallas kernels  10.2 us (11%)
    all_to_all x4, blocking collectives, swap(): lax.all_to_all(value, AXES, split_axis=0, concat_axis=0, axis_index_group...  83.5 us
    pallas_call x1, Pallas kernels, project(): pl.pallas_call(project_kernel, out_shape=vmem((4, 4 * ROWS, D)), in_specs...  6.93 us

profile of v2, /device:TPU:56, one launch (start us, length us, event | category | flops | bytes accessed | tf_op | source)
XLA Modules:
  0.0 93.7 jit_solution(15221415328381172107)
XLA Ops:
  0.0 1.8 %activate.1 = bf16[4,4,32,896]{3,2,1,0:T(8,128)(2,1)S(1)} custom-call(bf16[32,14336]{1,0:T(8,128)(2,1)} %gate_ref.1, bf16[32,14336]{1,0:T(8,128)(2,1)} %up_ref.1), custom_call_target="tpu_custom_call" | custom-call | tf_op jit(solution)/shard_map/activate/pallas_call | solution.py:94
  1.8 28.1 %all_to_all.20.came = bf16[4,4,32,896]{3,2,1,0:T(8,128)(2,1)S(1)} all-to-all(bf16[4,4,32,896]{3,2,1,0:T(8,128)(2,1)S(1)} %activate.1), channel_id=1, replica_groups={{5,6,9,10},{7,4,11,8},{13,14,257,258},{15,12,259,256},{16,17,20,21},{18..., dimensions={0} | all-to-all | bytes 1835008 | tf_op jit(solution)/shard_map/all_to_all | solution.py:37
  29.9 0.1 regroup.1
  30.0 11.7 %all_to_all.21.hidden = bf16[4,128,896]{2,1,0:T(8,128)(2,1)S(1)} all-to-all(bf16[4,128,896]{2,1,0:T(8,128)(2,1)S(1)} %regroup.1), channel_id=1, replica_groups={{0,1,4,5},{2,3,6,7},{8,9,12,13},{10,11,14,15},{21,22,25,26},{23,20,27,2..., dimensions={0} | all-to-all | bytes 1835008 | tf_op jit(solution)/shard_map/all_to_all | solution.py:37
  41.7 6.9 %project.1 = bf16[4,128,4096]{2,1,0:T(8,128)(2,1)S(1)} custom-call(bf16[4,128,896]{2,1,0:T(8,128)(2,1)S(1)} %all_to_all.21.hidden, bf16[896,4096]{1,0:T(8,128)(2,1)} %weight.1), custom_call_target="tpu_custom_call" | custom-call | flops 3758096384 | bytes 7340032 | tf_op jit(solution)/shard_map/project/pallas_call | solution.py:147
  48.6 29.4 %all_to_all.22.parts = bf16[4,128,4096]{2,1,0:T(8,128)(2,1)S(1)} all-to-all(bf16[4,128,4096]{2,1,0:T(8,128)(2,1)S(1)} %project.1), channel_id=1, replica_groups={{0,1,4,5},{2,3,6,7},{8,9,12,13},{10,11,14,15},{21,22,25,26},{23,20,27,2..., dimensions={0} | all-to-all | bytes 8388608 | tf_op jit(solution)/shard_map/all_to_all | solution.py:37
  78.0 0.5 add_up.2
  78.5 14.3 %all_to_all.23.parts = bf16[4,32,4096]{2,1,0:T(8,128)(2,1)S(1)} all-to-all(bf16[4,32,4096]{2,1,0:T(8,128)(2,1)S(1)} %bitcast.1), channel_id=1, replica_groups={{5,6,9,10},{7,4,11,8},{13,14,257,258},{15,12,259,256},{16,17,20,21},{18..., dimensions={0} | all-to-all | bytes 2097152 | tf_op jit(solution)/shard_map/all_to_all | solution.py:37
  92.9 0.9 add_up.3

commit v3 on v2

--- a/solution.py
+++ b/solution.py
@@ -1,3 +1,5 @@
+import functools
+
 import jax
 import jax.numpy as jnp
 import numpy as np
@@ -127,67 +129,135 @@
 TILES = D // TILE
 
 
-def project_kernel(hidden, weight, out, held, sems):
+def inner_member():
+    dp, tensor = lax.axis_index("dp"), lax.axis_index("tensor")
+    core = lax.rem(dp, CORES)
+    return 2 * lax.rem(lax.div(tensor, X) + core, 2) + lax.rem(lax.rem(tensor, X) + core, 2)
+
+
+def flip(value, flipped):
+    return lax.bitwise_xor(value, jnp.int32(flipped))
+
+
+def first_terms_kernel(hidden, weight, held, diagonal, sems):
     copies = [
         pltpu.make_async_copy(
-            weight.at[:, TILE * tile : TILE * (tile + 1)], held.at[tile], sems.at[tile]
+            weight.at[:, TILE * tile : TILE * (tile + 1)],
+            held.at[:, TILE * tile : TILE * (tile + 1)],
+            sems.at[tile],
         )
         for tile in range(TILES)
     ]
     for copy in copies:
         copy.start()
-    rows = hidden[...].reshape(16 * ROWS, WIDTH)
+    rows = hidden[flip(inner_member(), 3)]
     for tile, copy in enumerate(copies):
         copy.wait()
-        terms = jnp.dot(rows, held[tile], preferred_element_type=jnp.float32)
-        out[:, :, TILE * tile : TILE * (tile + 1)] = terms.astype(jnp.bfloat16).reshape(4, 4 * ROWS, TILE)
-
-
-def project(hidden, weight):
-    return pl.pallas_call(
-        project_kernel,
-        out_shape=vmem((4, 4 * ROWS, D)),
+        columns = slice(TILE * tile, TILE * (tile + 1))
+        diagonal[:, columns] = jnp.dot(
+            rows, held[:, columns], preferred_element_type=jnp.float32
+        ).astype(jnp.bfloat16)
+
+
+def first_terms(hidden, weight):
+    return pl.pallas_call(
+        first_terms_kernel,
+        out_shape=[vmem((WIDTH, D)), vmem((4 * ROWS, D))],
         in_specs=[whole(), stays()],
-        out_specs=whole(),
-        scratch_shapes=[
-            pltpu.VMEM((TILES, WIDTH, TILE), jnp.bfloat16),
-            pltpu.SemaphoreType.DMA((TILES,)),
-        ],
-        cost_estimate=pl.CostEstimate(
-            flops=2 * 16 * ROWS * WIDTH * D, bytes_accessed=2 * WIDTH * D, transcendentals=0
-        ),
-        compiler_params=pltpu.CompilerParams(vmem_limit_bytes=16 * MIB),
-        name="project",
+        out_specs=[whole()] * 2,
+        scratch_shapes=[pltpu.SemaphoreType.DMA((TILES,))],
+        cost_estimate=pl.CostEstimate(flops=1, bytes_accessed=1, transcendentals=0),
+        compiler_params=pltpu.CompilerParams(vmem_limit_bytes=4 * MIB),
+        name="first_terms",
     )(in_vmem(hidden), in_hbm(weight))
 
 
-def add_kernel(parts, out):
+def terms_kernel(flipped, hidden, held, earlier, out):
+    del earlier
+    rows = hidden[flip(inner_member(), flipped)]
+    for tile in range(TILES):
+        columns = slice(TILE * tile, TILE * (tile + 1))
+        out[:, columns] = jnp.dot(
+            rows, held[:, columns], preferred_element_type=jnp.float32
+        ).astype(jnp.bfloat16)
+
+
+def terms_for(hidden, held, flipped, earlier):
+    return pl.pallas_call(
+        functools.partial(terms_kernel, flipped),
+        out_shape=vmem((4 * ROWS, D)),
+        in_specs=[whole(), whole(), pl.BlockSpec(memory_space=pl.ANY)],
+        out_specs=whole(),
+        cost_estimate=pl.CostEstimate(flops=1, bytes_accessed=1, transcendentals=0),
+        compiler_params=pltpu.CompilerParams(vmem_limit_bytes=4 * MIB),
+        name="terms",
+    )(in_vmem(hidden), in_vmem(held), earlier)
+
+
+def partners(flipped):
+    pairs = []
+    for group in squares(0):
+        pairs += [(group[m], group[m ^ flipped]) for m in range(4)]
+    return pairs
+
+
+def trade(value, flipped):
+    return lax.ppermute(value, AXES, partners(flipped))
+
+
+def add_kernel(*refs):
+    *parts, out = refs
+
     @pl.loop(0, TILES)
     def _(tile):
         columns = pl.ds(pl.multiple_of(tile * TILE, TILE), TILE)
+        total = parts[0][:, columns].astype(jnp.float32)
+        for part in parts[1:]:
+            total += part[:, columns].astype(jnp.float32)
+        out[:, columns] = total.astype(out.dtype)
+
+
+def add(dtype, *parts):
+    return pl.pallas_call(
+        add_kernel,
+        out_shape=pltpu.VMEM((4 * ROWS, D), dtype),
+        in_specs=[whole()] * len(parts),
+        out_specs=whole(),
+        cost_estimate=pl.CostEstimate(flops=1, bytes_accessed=1, transcendentals=0),
+        compiler_params=pltpu.CompilerParams(vmem_limit_bytes=4 * MIB),
+        name="add",
+    )(*(in_vmem(part) for part in parts))
+
+
+def outer_sum_kernel(parts, out):
+    for tile in range(TILES):
+        columns = slice(TILE * tile, TILE * (tile + 1))
         total = parts[0, :, columns].astype(jnp.float32)
         for member in range(1, 4):
             total += parts[member, :, columns].astype(jnp.float32)
         out[:, columns] = total.astype(jnp.bfloat16)
 
 
-def add_up(parts, out_shape):
-    return pl.pallas_call(
-        add_kernel,
-        out_shape=out_shape,
+def outer_sum(parts):
+    return pl.pallas_call(
+        outer_sum_kernel,
+        out_shape=jax.ShapeDtypeStruct((ROWS, D), jnp.bfloat16),
         in_specs=[whole()],
         out_specs=whole(),
         compiler_params=pltpu.CompilerParams(vmem_limit_bytes=4 * MIB),
-        name="add_up",
+        name="outer_sum",
     )(in_vmem(parts))
 
 
 def shards(gate_pre, up_pre, down_weight):
-    hidden = regroup(swap(activate(gate_pre, up_pre), 1))
-    terms = project(swap(hidden, 0), down_weight)
-    sums = add_up(swap(terms, 0), vmem((4 * ROWS, D)))
-    sums = swap(sums.reshape(4, ROWS, D), 1)
-    return add_up(sums, jax.ShapeDtypeStruct((ROWS, D), jnp.bfloat16))
+    hidden = swap(regroup(swap(activate(gate_pre, up_pre), 1)), 0)
+    held, diagonal = first_terms(hidden, down_weight)
+    beside = terms_for(hidden, held, 1, diagonal)
+    below = terms_for(hidden, held, 2, beside)
+    own = terms_for(hidden, held, 0, below)
+    sums = add(jnp.float32, own, trade(diagonal, 3))
+    sums = add(jnp.bfloat16, sums, trade(beside, 1), trade(below, 2))
+    return outer_sum(swap(sums.reshape(4, ROWS, D), 1))
 
 
 def solution(mesh):

time: 94.1 us -> 90.2 us (0.959)
  blocking collectives: 83.5 us -> 54.2 us
  waiting for transfers between devices: 0 us -> 15.5 us
  starting transfers between devices: 0 us -> 9.21 us
    all_to_all x4 -> x3, blocking collectives: 83.5 us -> 54.2 us  [swap(): lax.all_to_all(value, AXES, split_axis=0, concat_axis=0, axis_index_group...]
    ppermute x0 -> x3, waiting for transfers between devices: none -> 15.5 us  [trade(): return lax.ppermute(value, AXES, partners(flipped))]
    ppermute x0 -> x3, starting transfers between devices: none -> 9.21 us  [trade(): return lax.ppermute(value, AXES, partners(flipped))]
    pallas_call x3 -> x7, Pallas kernels: 8.34 us -> 8.97 us  [the longest x3 3.8 us: terms_for(): pl.pallas_call(functools.partial(terms_kernel, flipped), out_shape=vmem((...]
  transfers between devices with their start and end apart: 0 -> 3, of which waited for: 0 -> 3; matrix products, arithmetic and copies ran while one was open for 0% -> 0% of each run, Pallas kernels for 0% -> 4%
where the time goes in v3:
time: 90.2 us; the launch traced here: 89.9 us
  blocking collectives  54.2 us (60%)
  waiting for transfers between devices  15.5 us (17%)
  Pallas kernels  10.8 us (12%)
  starting transfers between devices  9.21 us (10%)
    all_to_all x3, blocking collectives, swap(): lax.all_to_all(value, AXES, split_axis=0, concat_axis=0, axis_index_group...  54.2 us
    ppermute x3, waiting for transfers between devices, trade(): return lax.ppermute(value, AXES, partners(flipped))  15.5 us
    ppermute x3, starting transfers between devices, trade(): return lax.ppermute(value, AXES, partners(flipped))  9.21 us
    pallas_call x3, Pallas kernels, terms_for(): pl.pallas_call(functools.partial(terms_kernel, flipped), out_shape=vmem((...  3.8 us
    pallas_call x1, Pallas kernels, first_terms(): pl.pallas_call(first_terms_kernel, out_shape=[vmem((WIDTH, D)), vmem((4 *...  3.74 us
  transfers between devices with their start and end apart: 3, of which 3 were waited for; matrix products, arithmetic and copies ran while one was open for 0% of the time, Pallas kernels for 4%

profile of v3, /device:TPU:56, one launch (start us, length us, event | category | flops | bytes accessed | tf_op | source)
XLA Modules:
  0.0 89.9 jit_solution(2441108792745226471)
XLA Ops:
  0.0 1.8 %activate.1 = bf16[4,4,32,896]{3,2,1,0:T(8,128)(2,1)S(1)} custom-call(bf16[32,14336]{1,0:T(8,128)(2,1)} %gate_ref.1, bf16[32,14336]{1,0:T(8,128)(2,1)} %up_ref.1), custom_call_target="tpu_custom_call" | custom-call | tf_op jit(solution)/shard_map/activate/pallas_call | solution.py:96
  1.8 28.1 %all_to_all.15.came = bf16[4,4,32,896]{3,2,1,0:T(8,128)(2,1)S(1)} all-to-all(bf16[4,4,32,896]{3,2,1,0:T(8,128)(2,1)S(1)} %activate.1), channel_id=1, replica_groups={{5,6,9,10},{7,4,11,8},{13,14,257,258},{15,12,259,256},{16,17,20,21},{18..., dimensions={0} | all-to-all | bytes 1835008 | tf_op jit(solution)/shard_map/all_to_all | solution.py:39
  29.9 0.1 regroup.1
  30.0 11.7 %all_to_all.16.hidden = bf16[4,128,896]{2,1,0:T(8,128)(2,1)S(1)} all-to-all(bf16[4,128,896]{2,1,0:T(8,128)(2,1)S(1)} %regroup.1), channel_id=1, replica_groups={{0,1,4,5},{2,3,6,7},{8,9,12,13},{10,11,14,15},{21,22,25,26},{23,20,27,2..., dimensions={0} | all-to-all | bytes 1835008 | tf_op jit(solution)/shard_map/all_to_all | solution.py:39
  41.7 3.7 %first_terms.1 = (bf16[896,4096]{1,0:T(8,128)(2,1)S(1)}, bf16[128,4096]{1,0:T(8,128)(2,1)S(1)}) custom-call(bf16[4,128,896]{2,1,0:T(8,128)(2,1)S(1)} %all_to_all.16.hidden, bf16[896,4096]{1,0:T(8,128)(2,1)} %weight.1), custom_call_target="tpu_custom_call" | custom-call | flops 1 | bytes 1 | tf_op jit(solution)/shard_map/first_terms/pallas_call | solution.py:163
  45.4 2.8 %collective-permute-start = (bf16[128,4096]{1,0:T(8,128)(2,1)S(1)}, bf16[128,4096]{1,0:T(8,128)(2,1)S(1)}, u32[]{:S(2)}, u32[]{:S(2)}) collective-permute-start(bf16[128,4096]{1,0:T(8,128)(2,1)S(1)} %get-tuple-element.8.earlier), channel_id=1, source_target_pairs={{0,5},{1,4},{4,1},{5,0},{2,7},{3,6},{6,3},{7,2},{8,13},{9,12},{12,... | collective-permute-start | bytes 3145736 | tf_op jit(solution)/shard_map/ppermute | solution.py:205
  48.2 1.3 %terms.3.earlier = bf16[128,4096]{1,0:T(8,128)(2,1)S(1)} custom-call(bf16[4,128,896]{2,1,0:T(8,128)(2,1)S(1)} %all_to_all.16.hidden, bf16[896,4096]{1,0:T(8,128)(2,1)S(1)} %get-tuple-element.7.held, bf16[128,4096]{1,0:T(8,128)(2,1)S(1)} %get-tuple-element.8.earlier), custom_call_target="tpu_custom_call" | custom-call | flops 1 | bytes 1 | tf_op jit(solution)/shard_map/terms/pallas_call | solution.py:186
  49.5 1.3 %terms.4.earlier = bf16[128,4096]{1,0:T(8,128)(2,1)S(1)} custom-call(bf16[4,128,896]{2,1,0:T(8,128)(2,1)S(1)} %all_to_all.16.hidden, bf16[896,4096]{1,0:T(8,128)(2,1)S(1)} %get-tuple-element.7.held, bf16[128,4096]{1,0:T(8,128)(2,1)S(1)} %terms.3.earlier), custom_call_target="tpu_custom_call" | custom-call | flops 1 | bytes 1 | tf_op jit(solution)/shard_map/terms/pallas_call | solution.py:186
  50.8 3.4 %collective-permute-start.2 = (bf16[128,4096]{1,0:T(8,128)(2,1)S(1)}, bf16[128,4096]{1,0:T(8,128)(2,1)S(1)}, u32[]{:S(2)}, u32[]{:S(2)}) collective-permute-start(bf16[128,4096]{1,0:T(8,128)(2,1)S(1)} %terms.4.earlier), channel_id=1, source_target_pairs={{0,4},{1,5},{4,0},{5,1},{2,6},{3,7},{6,2},{7,3},{8,12},{9,13},{12,... | collective-permute-start | bytes 3145736 | tf_op jit(solution)/shard_map/ppermute | solution.py:205
  54.2 3.0 %collective-permute-start.1 = (bf16[128,4096]{1,0:T(8,128)(2,1)S(1)}, bf16[128,4096]{1,0:T(8,128)(2,1)S(1)}, u32[]{:S(2)}, u32[]{:S(2)}) collective-permute-start(bf16[128,4096]{1,0:T(8,128)(2,1)S(1)} %terms.3.earlier), channel_id=1, source_target_pairs={{0,1},{1,0},{4,5},{5,4},{2,3},{3,2},{6,7},{7,6},{8,9},{9,8},{12,13... | collective-permute-start | bytes 3145736 | tf_op jit(solution)/shard_map/ppermute | solution.py:205
  57.2 1.3 %terms.5.refs_0_ = bf16[128,4096]{1,0:T(8,128)(2,1)S(1)} custom-call(bf16[4,128,896]{2,1,0:T(8,128)(2,1)S(1)} %all_to_all.16.hidden, bf16[896,4096]{1,0:T(8,128)(2,1)S(1)} %get-tuple-element.7.held, bf16[128,4096]{1,0:T(8,128)(2,1)S(1)} %terms.4.earlier), custom_call_target="tpu_custom_call" | custom-call | flops 1 | bytes 1 | tf_op jit(solution)/shard_map/terms/pallas_call | solution.py:186
  58.5 4.6 %collective-permute-done.refs_1_ = bf16[128,4096]{1,0:T(8,128)(2,1)S(1)} collective-permute-done((bf16[128,4096]{1,0:T(8,128)(2,1)S(1)}, bf16[128,4096]{1,0:T(8,128)(2,1)S(1)}, u32[]{:S(2)}, u32[]{:S(2)}) %collective-permute-start) | collective-permute-done | bytes 1048608 | tf_op jit(solution)/shard_map/ppermute | solution.py:205
  63.1 0.2 add.2.refs_0_
  63.4 10.4 %collective-permute-done.2.refs_2_ = bf16[128,4096]{1,0:T(8,128)(2,1)S(1)} collective-permute-done((bf16[128,4096]{1,0:T(8,128)(2,1)S(1)}, bf16[128,4096]{1,0:T(8,128)(2,1)S(1)}, u32[]{:S(2)}, u32[]{:S(2)}) %collective-permute-start.2) | collective-permute-done | bytes 1048608 | tf_op jit(solution)/shard_map/ppermute | solution.py:205
  73.7 0.5 collective-permute-done.1.refs_1_
  74.2 0.4 add.3
  74.6 14.4 %all_to_all.17.parts = bf16[4,32,4096]{2,1,0:T(8,128)(2,1)S(1)} all-to-all(bf16[4,32,4096]{2,1,0:T(8,128)(2,1)S(1)} %bitcast.1), channel_id=1, replica_groups={{5,6,9,10},{7,4,11,8},{13,14,257,258},{15,12,259,256},{16,17,20,21},{18..., dimensions={0} | all-to-all | bytes 2097152 | tf_op jit(solution)/shard_map/all_to_all | solution.py:39
  89.0 0.8 outer_sum.1
Async XLA Ops:
  45.4 17.7 %collective-permute-start = (bf16[128,4096]{1,0:T(8,128)(2,1)S(1)}, bf16[128,4096]{1,0:T(8,128)(2,1)S(1)}, u32[]{:S(2)}, u32[]{:S(2)}) collective-permute-start(bf16[128,4096]{1,0:T(8,128)(2,1)S(1)} %get-tuple-element.8.earlier), channel_id=1, source_target_pairs={{0,5},{1,4},{4,1},{5,0},{2,7},{3,6},{6,3},{7,2},{8,13},{9,12},{12,... | collective-permute-start | bytes 3145736 | tf_op jit(solution)/shard_map/ppermute | solution.py:205
  50.8 23.0 %collective-permute-start.2 = (bf16[128,4096]{1,0:T(8,128)(2,1)S(1)}, bf16[128,4096]{1,0:T(8,128)(2,1)S(1)}, u32[]{:S(2)}, u32[]{:S(2)}) collective-permute-start(bf16[128,4096]{1,0:T(8,128)(2,1)S(1)} %terms.4.earlier), channel_id=1, source_target_pairs={{0,4},{1,5},{4,0},{5,1},{2,6},{3,7},{6,2},{7,3},{8,12},{9,13},{12,... | collective-permute-start | bytes 3145736 | tf_op jit(solution)/shard_map/ppermute | solution.py:205
  54.2 20.1 %collective-permute-start.1 = (bf16[128,4096]{1,0:T(8,128)(2,1)S(1)}, bf16[128,4096]{1,0:T(8,128)(2,1)S(1)}, u32[]{:S(2)}, u32[]{:S(2)}) collective-permute-start(bf16[128,4096]{1,0:T(8,128)(2,1)S(1)} %terms.3.earlier), channel_id=1, source_target_pairs={{0,1},{1,0},{4,5},{5,4},{2,3},{3,2},{6,7},{7,6},{8,9},{9,8},{12,13... | collective-permute-start | bytes 3145736 | tf_op jit(solution)/shard_map/ppermute | solution.py:205

commit v4 on v3

--- a/solution.py
+++ b/solution.py
@@ -1,5 +1,3 @@
-import functools
-
 import jax
 import jax.numpy as jnp
 import numpy as np
@@ -24,7 +22,7 @@
     groups = []
     for zh, y, c, zl, x in np.ndindex(Z_HI, Y, CORES, Z_LO, X):
         z, shift = zh * Z_LO + zl, c ^ outer
-        z0, x0 = pair_base(z, shift), pair_base(x, shift)
+        z0, x0 = pair_base(z, 1 - shift), pair_base(x, shift)
         if (z0, x0) != (z, x) and (z0 % Z, x0 % X) != (z, x):
             continue
         group = []
@@ -72,7 +70,7 @@
     copies = []
     for i, (oz, ox) in enumerate(BITS):
         for j, (iz, ix) in enumerate(BITS):
-            to_z = member(member(zl + 4, 1 - core, oz), core, iz)
+            to_z = member(member(zl + 4, core, oz), 1 - core, iz)
             to_x = member(member(x + 4, 1 - core, ox), core, ix)
             block = lax.rem(to_z, Z_LO) * X + lax.rem(to_x, X)
             columns = pl.ds(pl.multiple_of(block * WIDTH, 128), WIDTH)
@@ -108,38 +106,39 @@
     )(in_hbm(gate_pre), in_hbm(up_pre))
 
 
-def regroup_kernel(came, out):
-    for i in range(4):
-        for j in range(4):
-            out[j, ROWS * i : ROWS * (i + 1), :] = came[i, j]
-
-
-def regroup(came):
-    return pl.pallas_call(
-        regroup_kernel,
-        out_shape=vmem((4, 4 * ROWS, WIDTH)),
-        in_specs=[whole()],
-        out_specs=whole(),
-        compiler_params=pltpu.CompilerParams(vmem_limit_bytes=4 * MIB),
-        name="regroup",
-    )(in_vmem(came))
-
-
-TILE = 512
-TILES = D // TILE
-
-
 def inner_member():
     dp, tensor = lax.axis_index("dp"), lax.axis_index("tensor")
     core = lax.rem(dp, CORES)
-    return 2 * lax.rem(lax.div(tensor, X) + core, 2) + lax.rem(lax.rem(tensor, X) + core, 2)
+    return 2 * lax.rem(lax.div(tensor, X) + 1 - core, 2) + lax.rem(lax.rem(tensor, X) + core, 2)
 
 
 def flip(value, flipped):
     return lax.bitwise_xor(value, jnp.int32(flipped))
 
 
-def first_terms_kernel(hidden, weight, held, diagonal, sems):
+def regroup_kernel(came, *outs):
+    me = inner_member()
+    for flipped, out in enumerate(outs):
+        for i in range(4):
+            out[ROWS * i : ROWS * (i + 1), :] = came[i, flip(me, flipped)]
+
+
+def regroup(came):
+    return pl.pallas_call(
+        regroup_kernel,
+        out_shape=[vmem((4 * ROWS, WIDTH))] * 4,
+        in_specs=[whole()],
+        out_specs=[whole()] * 4,
+        compiler_params=pltpu.CompilerParams(vmem_limit_bytes=4 * MIB),
+        name="regroup",
+    )(in_vmem(came))
+
+
+TILE = 512
+TILES = D // TILE
+
+
+def first_terms_kernel(rows, weight, held, out, sems):
     copies = [
         pltpu.make_async_copy(
             weight.at[:, TILE * tile : TILE * (tile + 1)],
@@ -150,16 +149,15 @@
     ]
     for copy in copies:
         copy.start()
-    rows = hidden[flip(inner_member(), 3)]
     for tile, copy in enumerate(copies):
         copy.wait()
         columns = slice(TILE * tile, TILE * (tile + 1))
-        diagonal[:, columns] = jnp.dot(
-            rows, held[:, columns], preferred_element_type=jnp.float32
+        out[:, columns] = jnp.dot(
+            rows[...], held[:, columns], preferred_element_type=jnp.float32
         ).astype(jnp.bfloat16)
 
 
-def first_terms(hidden, weight):
+def first_terms(rows, weight):
     return pl.pallas_call(
         first_terms_kernel,
         out_shape=[vmem((WIDTH, D)), vmem((4 * ROWS, D))],
@@ -169,29 +167,28 @@
         cost_estimate=pl.CostEstimate(flops=1, bytes_accessed=1, transcendentals=0),
         compiler_params=pltpu.CompilerParams(vmem_limit_bytes=4 * MIB),
         name="first_terms",
-    )(in_vmem(hidden), in_hbm(weight))
-
-
-def terms_kernel(flipped, hidden, held, earlier, out):
+    )(in_vmem(rows), in_hbm(weight))
+
+
+def terms_kernel(rows, held, earlier, out):
     del earlier
-    rows = hidden[flip(inner_member(), flipped)]
     for tile in range(TILES):
         columns = slice(TILE * tile, TILE * (tile + 1))
         out[:, columns] = jnp.dot(
-            rows, held[:, columns], preferred_element_type=jnp.float32
+            rows[...], held[:, columns], preferred_element_type=jnp.float32
         ).astype(jnp.bfloat16)
 
 
-def terms_for(hidden, held, flipped, earlier):
-    return pl.pallas_call(
-        functools.partial(terms_kernel, flipped),
+def terms_for(rows, held, earlier):
+    return pl.pallas_call(
+        terms_kernel,
         out_shape=vmem((4 * ROWS, D)),
         in_specs=[whole(), whole(), pl.BlockSpec(memory_space=pl.ANY)],
         out_specs=whole(),
         cost_estimate=pl.CostEstimate(flops=1, bytes_accessed=1, transcendentals=0),
         compiler_params=pltpu.CompilerParams(vmem_limit_bytes=4 * MIB),
         name="terms",
-    )(in_vmem(hidden), in_vmem(held), earlier)
+    )(in_vmem(rows), in_vmem(held), earlier)
 
 
 def partners(flipped):
@@ -250,11 +247,12 @@
 
 
 def shards(gate_pre, up_pre, down_weight):
-    hidden = swap(regroup(swap(activate(gate_pre, up_pre), 1)), 0)
-    held, diagonal = first_terms(hidden, down_weight)
-    beside = terms_for(hidden, held, 1, diagonal)
-    below = terms_for(hidden, held, 2, beside)
-    own = terms_for(hidden, held, 0, below)
+    own, beside, below, diagonal = regroup(swap(activate(gate_pre, up_pre), 1))
+    beside, below, diagonal = trade(beside, 1), trade(below, 2), trade(diagonal, 3)
+    held, own = first_terms(own, down_weight)
+    diagonal = terms_for(diagonal, held, own)
+    beside = terms_for(beside, held, diagonal)
+    below = terms_for(below, held, beside)
     sums = add(jnp.float32, own, trade(diagonal, 3))
     sums = add(jnp.bfloat16, sums, trade(beside, 1), trade(below, 2))
     return outer_sum(swap(sums.reshape(4, ROWS, D), 1))

time: 90.2 us -> 88.6 us (0.982)
  blocking collectives: 54.2 us -> 28.3 us
  starting transfers between devices: 9.21 us -> 32.1 us
  waiting for transfers between devices: 15.5 us -> 16.8 us
    all_to_all x3 -> x2, blocking collectives: 54.2 us -> 28.3 us  [swap(): lax.all_to_all(value, AXES, split_axis=0, concat_axis=0, axis_index_group...]
    ppermute x3 -> x6, starting transfers between devices: 9.21 us -> 32.1 us  [trade(): return lax.ppermute(value, AXES, partners(flipped))]
    ppermute x3 -> x6, waiting for transfers between devices: 15.5 us -> 16.8 us  [trade(): return lax.ppermute(value, AXES, partners(flipped))]
  transfers between devices with their start and end apart: 3 -> 6, of which waited for: 3 -> 3; matrix products, arithmetic and copies ran while one was open for 0% -> 0% of each run, Pallas kernels for 4% -> 9%
where the time goes in v4:
time: 88.6 us; the launch traced here: 88.2 us
  starting transfers between devices  32.1 us (36%)
  blocking collectives  28.3 us (32%)
  waiting for transfers between devices  16.8 us (19%)
  Pallas kernels  10.9 us (12%)
    ppermute x6, starting transfers between devices, trade(): return lax.ppermute(value, AXES, partners(flipped))  32.1 us
    all_to_all x2, blocking collectives, swap(): lax.all_to_all(value, AXES, split_axis=0, concat_axis=0, axis_index_group...  28.3 us
    ppermute x6, waiting for transfers between devices, trade(): return lax.ppermute(value, AXES, partners(flipped))  16.8 us
    pallas_call x3, Pallas kernels, terms_for(): pl.pallas_call(terms_kernel, out_shape=vmem((4 * ROWS, D)), in_specs=[who...  3.81 us
    pallas_call x1, Pallas kernels, first_terms(): pl.pallas_call(first_terms_kernel, out_shape=[vmem((WIDTH, D)), vmem((4 *...  3.76 us
    pallas_call x1, Pallas kernels, activate(): pl.pallas_call(activate_kernel, out_shape=vmem(shape), in_specs=[stays()]...  1.79 us
  transfers between devices with their start and end apart: 6, of which 3 were waited for; matrix products, arithmetic and copies ran while one was open for 0% of the time, Pallas kernels for 9%

profile of v4, /device:TPU:56, one launch (start us, length us, event | category | flops | bytes accessed | tf_op | source)
XLA Modules:
  0.0 88.2 jit_solution(5415231561213429379)
XLA Ops:
  0.0 1.8 %activate.1 = bf16[4,4,32,896]{3,2,1,0:T(8,128)(2,1)S(1)} custom-call(bf16[32,14336]{1,0:T(8,128)(2,1)} %gate_ref.1, bf16[32,14336]{1,0:T(8,128)(2,1)} %up_ref.1), custom_call_target="tpu_custom_call" | custom-call | tf_op jit(solution)/shard_map/activate/pallas_call | solution.py:94
  1.8 14.3 %all_to_all.10.came = bf16[4,4,32,896]{3,2,1,0:T(8,128)(2,1)S(1)} all-to-all(bf16[4,4,32,896]{3,2,1,0:T(8,128)(2,1)S(1)} %activate.1), channel_id=1, replica_groups={{1,2,5,6},{3,0,7,4},{9,10,13,14},{11,8,15,12},{20,21,24,25},{22,23,26,2..., dimensions={0} | all-to-all | bytes 1835008 | tf_op jit(solution)/shard_map/all_to_all | solution.py:37
  16.1 0.1 regroup.1
  16.2 17.0 %collective-permute-start = (bf16[128,896]{1,0:T(8,128)(2,1)S(1)}, bf16[128,896]{1,0:T(8,128)(2,1)S(1)}, u32[]{:S(2)}, u32[]{:S(2)}) collective-permute-start(bf16[128,896]{1,0:T(8,128)(2,1)S(1)} %get-tuple-element.13), channel_id=1, source_target_pairs={{4,9},{5,8},{8,5},{9,4},{6,11},{7,10},{10,7},{11,6},{12,257},{13,2... | collective-permute-start | bytes 688136 | tf_op jit(solution)/shard_map/ppermute | solution.py:202
  33.2 2.8 %collective-permute-start.2 = (bf16[128,896]{1,0:T(8,128)(2,1)S(1)}, bf16[128,896]{1,0:T(8,128)(2,1)S(1)}, u32[]{:S(2)}, u32[]{:S(2)}) collective-permute-start(bf16[128,896]{1,0:T(8,128)(2,1)S(1)} %get-tuple-element.15), channel_id=1, source_target_pairs={{4,5},{5,4},{8,9},{9,8},{6,7},{7,6},{10,11},{11,10},{12,13},{13,12... | collective-permute-start | bytes 688136 | tf_op jit(solution)/shard_map/ppermute | solution.py:202
  36.0 1.9 %collective-permute-start.4 = (bf16[128,896]{1,0:T(8,128)(2,1)S(1)}, bf16[128,896]{1,0:T(8,128)(2,1)S(1)}, u32[]{:S(2)}, u32[]{:S(2)}) collective-permute-start(bf16[128,896]{1,0:T(8,128)(2,1)S(1)} %get-tuple-element.16), channel_id=1, source_target_pairs={{4,8},{5,9},{8,4},{9,5},{6,10},{7,11},{10,6},{11,7},{12,256},{13,2... | collective-permute-start | bytes 688136 | tf_op jit(solution)/shard_map/ppermute | solution.py:202
  37.9 3.8 %first_terms.1 = (bf16[896,4096]{1,0:T(8,128)(2,1)S(1)}, bf16[128,4096]{1,0:T(8,128)(2,1)S(1)}) custom-call(bf16[128,896]{1,0:T(8,128)(2,1)S(1)} %get-tuple-element.11.rows, bf16[896,4096]{1,0:T(8,128)(2,1)} %weight.1), custom_call_target="tpu_custom_call" | custom-call | flops 1 | bytes 1 | tf_op jit(solution)/shard_map/first_terms/pallas_call | solution.py:161
  41.7 0.0 collective-permute-done.rows
  41.7 1.3 %terms.3.earlier = bf16[128,4096]{1,0:T(8,128)(2,1)S(1)} custom-call(bf16[128,896]{1,0:T(8,128)(2,1)S(1)} %collective-permute-done.rows, bf16[896,4096]{1,0:T(8,128)(2,1)S(1)} %get-tuple-element.14.held, bf16[128,4096]{1,0:T(8,128)(2,1)S(1)} %get-tuple-element.12.earlier.refs_0_), custom_call_target="tpu_custom_call" | custom-call | flops 1 | bytes 1 | tf_op jit(solution)/shard_map/terms/pallas_call | solution.py:183
  43.0 5.7 %collective-permute-start.1 = (bf16[128,4096]{1,0:T(8,128)(2,1)S(1)}, bf16[128,4096]{1,0:T(8,128)(2,1)S(1)}, u32[]{:S(2)}, u32[]{:S(2)}) collective-permute-start(bf16[128,4096]{1,0:T(8,128)(2,1)S(1)} %terms.3.earlier), channel_id=1, source_target_pairs={{4,9},{5,8},{8,5},{9,4},{6,11},{7,10},{10,7},{11,6},{12,257},{13,2... | collective-permute-start | bytes 3145736 | tf_op jit(solution)/shard_map/ppermute | solution.py:202
  48.7 0.0 collective-permute-done.2.rows
  48.7 1.3 %terms.4.earlier = bf16[128,4096]{1,0:T(8,128)(2,1)S(1)} custom-call(bf16[128,896]{1,0:T(8,128)(2,1)S(1)} %collective-permute-done.2.rows, bf16[896,4096]{1,0:T(8,128)(2,1)S(1)} %get-tuple-element.14.held, bf16[128,4096]{1,0:T(8,128)(2,1)S(1)} %terms.3.earlier), custom_call_target="tpu_custom_call" | custom-call | flops 1 | bytes 1 | tf_op jit(solution)/shard_map/terms/pallas_call | solution.py:183
  50.0 0.0 collective-permute-done.4.rows
  50.0 1.3 %terms.5 = bf16[128,4096]{1,0:T(8,128)(2,1)S(1)} custom-call(bf16[128,896]{1,0:T(8,128)(2,1)S(1)} %collective-permute-done.4.rows, bf16[896,4096]{1,0:T(8,128)(2,1)S(1)} %get-tuple-element.14.held, bf16[128,4096]{1,0:T(8,128)(2,1)S(1)} %terms.4.earlier), custom_call_target="tpu_custom_call" | custom-call | flops 1 | bytes 1 | tf_op jit(solution)/shard_map/terms/pallas_call | solution.py:183
  51.3 1.9 %collective-permute-start.5 = (bf16[128,4096]{1,0:T(8,128)(2,1)S(1)}, bf16[128,4096]{1,0:T(8,128)(2,1)S(1)}, u32[]{:S(2)}, u32[]{:S(2)}) collective-permute-start(bf16[128,4096]{1,0:T(8,128)(2,1)S(1)} %terms.5), channel_id=1, source_target_pairs={{4,8},{5,9},{8,4},{9,5},{6,10},{7,11},{10,6},{11,7},{12,256},{13,2... | collective-permute-start | bytes 3145736 | tf_op jit(solution)/shard_map/ppermute | solution.py:202
  53.2 2.8 %collective-permute-start.3 = (bf16[128,4096]{1,0:T(8,128)(2,1)S(1)}, bf16[128,4096]{1,0:T(8,128)(2,1)S(1)}, u32[]{:S(2)}, u32[]{:S(2)}) collective-permute-start(bf16[128,4096]{1,0:T(8,128)(2,1)S(1)} %terms.4.earlier), channel_id=1, source_target_pairs={{4,5},{5,4},{8,9},{9,8},{6,7},{7,6},{10,11},{11,10},{12,13},{13,12... | collective-permute-start | bytes 3145736 | tf_op jit(solution)/shard_map/ppermute | solution.py:202
  56.0 5.9 %collective-permute-done.1.refs_1_ = bf16[128,4096]{1,0:T(8,128)(2,1)S(1)} collective-permute-done((bf16[128,4096]{1,0:T(8,128)(2,1)S(1)}, bf16[128,4096]{1,0:T(8,128)(2,1)S(1)}, u32[]{:S(2)}, u32[]{:S(2)}) %collective-permute-start.1) | collective-permute-done | bytes 1048608 | tf_op jit(solution)/shard_map/ppermute | solution.py:202
  61.9 0.2 add.2.refs_0_
  62.1 10.6 %collective-permute-done.5.refs_2_ = bf16[128,4096]{1,0:T(8,128)(2,1)S(1)} collective-permute-done((bf16[128,4096]{1,0:T(8,128)(2,1)S(1)}, bf16[128,4096]{1,0:T(8,128)(2,1)S(1)}, u32[]{:S(2)}, u32[]{:S(2)}) %collective-permute-start.5) | collective-permute-done | bytes 1048608 | tf_op jit(solution)/shard_map/ppermute | solution.py:202
  72.7 0.3 collective-permute-done.3.refs_1_
  73.0 0.4 add.3
  73.4 13.9 %all_to_all.11.parts = bf16[4,32,4096]{2,1,0:T(8,128)(2,1)S(1)} all-to-all(bf16[4,32,4096]{2,1,0:T(8,128)(2,1)S(1)} %bitcast.1), channel_id=1, replica_groups={{1,2,5,6},{3,0,7,4},{9,10,13,14},{11,8,15,12},{20,21,24,25},{22,23,26,2..., dimensions={0} | all-to-all | bytes 2097152 | tf_op jit(solution)/shard_map/all_to_all | solution.py:37
  87.3 0.8 outer_sum.1
Async XLA Ops:
  16.2 25.5 %collective-permute-start = (bf16[128,896]{1,0:T(8,128)(2,1)S(1)}, bf16[128,896]{1,0:T(8,128)(2,1)S(1)}, u32[]{:S(2)}, u32[]{:S(2)}) collective-permute-start(bf16[128,896]{1,0:T(8,128)(2,1)S(1)} %get-tuple-element.13), channel_id=1, source_target_pairs={{4,9},{5,8},{8,5},{9,4},{6,11},{7,10},{10,7},{11,6},{12,257},{13,2... | collective-permute-start | bytes 688136 | tf_op jit(solution)/shard_map/ppermute | solution.py:202
  33.2 15.5 %collective-permute-start.2 = (bf16[128,896]{1,0:T(8,128)(2,1)S(1)}, bf16[128,896]{1,0:T(8,128)(2,1)S(1)}, u32[]{:S(2)}, u32[]{:S(2)}) collective-permute-start(bf16[128,896]{1,0:T(8,128)(2,1)S(1)} %get-tuple-element.15), channel_id=1, source_target_pairs={{4,5},{5,4},{8,9},{9,8},{6,7},{7,6},{10,11},{11,10},{12,13},{13,12... | collective-permute-start | bytes 688136 | tf_op jit(solution)/shard_map/ppermute | solution.py:202
  36.0 14.0 %collective-permute-start.4 = (bf16[128,896]{1,0:T(8,128)(2,1)S(1)}, bf16[128,896]{1,0:T(8,128)(2,1)S(1)}, u32[]{:S(2)}, u32[]{:S(2)}) collective-permute-start(bf16[128,896]{1,0:T(8,128)(2,1)S(1)} %get-tuple-element.16), channel_id=1, source_target_pairs={{4,8},{5,9},{8,4},{9,5},{6,10},{7,11},{10,6},{11,7},{12,256},{13,2... | collective-permute-start | bytes 688136 | tf_op jit(solution)/shard_map/ppermute | solution.py:202
  43.0 18.9 %collective-permute-start.1 = (bf16[128,4096]{1,0:T(8,128)(2,1)S(1)}, bf16[128,4096]{1,0:T(8,128)(2,1)S(1)}, u32[]{:S(2)}, u32[]{:S(2)}) collective-permute-start(bf16[128,4096]{1,0:T(8,128)(2,1)S(1)} %terms.3.earlier), channel_id=1, source_target_pairs={{4,9},{5,8},{8,5},{9,4},{6,11},{7,10},{10,7},{11,6},{12,257},{13,2... | collective-permute-start | bytes 3145736 | tf_op jit(solution)/shard_map/ppermute | solution.py:202
  51.3 21.5 %collective-permute-start.5 = (bf16[128,4096]{1,0:T(8,128)(2,1)S(1)}, bf16[128,4096]{1,0:T(8,128)(2,1)S(1)}, u32[]{:S(2)}, u32[]{:S(2)}) collective-permute-start(bf16[128,4096]{1,0:T(8,128)(2,1)S(1)} %terms.5), channel_id=1, source_target_pairs={{4,8},{5,9},{8,4},{9,5},{6,10},{7,11},{10,6},{11,7},{12,256},{13,2... | collective-permute-start | bytes 3145736 | tf_op jit(solution)/shard_map/ppermute | solution.py:202
  53.2 19.8 %collective-permute-start.3 = (bf16[128,4096]{1,0:T(8,128)(2,1)S(1)}, bf16[128,4096]{1,0:T(8,128)(2,1)S(1)}, u32[]{:S(2)}, u32[]{:S(2)}) collective-permute-start(bf16[128,4096]{1,0:T(8,128)(2,1)S(1)} %terms.4.earlier), channel_id=1, source_target_pairs={{4,5},{5,4},{8,9},{9,8},{6,7},{7,6},{10,11},{11,10},{12,13},{13,12... | collective-permute-start | bytes 3145736 | tf_op jit(solution)/shard_map/ppermute | solution.py:202

commit v5 on v4

--- a/solution.py
+++ b/solution.py
@@ -248,11 +248,11 @@
 
 def shards(gate_pre, up_pre, down_weight):
     own, beside, below, diagonal = regroup(swap(activate(gate_pre, up_pre), 1))
-    beside, below, diagonal = trade(beside, 1), trade(below, 2), trade(diagonal, 3)
-    held, own = first_terms(own, down_weight)
-    diagonal = terms_for(diagonal, held, own)
+    diagonal, beside, below = trade(diagonal, 3), trade(beside, 1), trade(below, 2)
+    held, diagonal = first_terms(diagonal, down_weight)
     beside = terms_for(beside, held, diagonal)
     below = terms_for(below, held, beside)
+    own = terms_for(own, held, below)
     sums = add(jnp.float32, own, trade(diagonal, 3))
     sums = add(jnp.bfloat16, sums, trade(beside, 1), trade(below, 2))
     return outer_sum(swap(sums.reshape(4, ROWS, D), 1))

time: 88.6 us -> 87.3 us (0.985)
  waiting for transfers between devices: 16.8 us -> 15.5 us
    ppermute x6, waiting for transfers between devices: 16.8 us -> 15.5 us  [trade(): return lax.ppermute(value, AXES, partners(flipped))]
where the time goes in v5:
time: 87.3 us; the launch traced here: 86.9 us
  starting transfers between devices  32.1 us (37%)
  blocking collectives  28.2 us (32%)
  waiting for transfers between devices  15.5 us (18%)
  Pallas kernels  10.9 us (12%)
    ppermute x6, starting transfers between devices, trade(): return lax.ppermute(value, AXES, partners(flipped))  32.1 us
    all_to_all x2, blocking collectives, swap(): lax.all_to_all(value, AXES, split_axis=0, concat_axis=0, axis_index_group...  28.2 us
    ppermute x6, waiting for transfers between devices, trade(): return lax.ppermute(value, AXES, partners(flipped))  15.5 us
    pallas_call x3, Pallas kernels, terms_for(): pl.pallas_call(terms_kernel, out_shape=vmem((4 * ROWS, D)), in_specs=[who...  3.81 us
    pallas_call x1, Pallas kernels, first_terms(): pl.pallas_call(first_terms_kernel, out_shape=[vmem((WIDTH, D)), vmem((4 *...  3.78 us
    pallas_call x1, Pallas kernels, activate(): pl.pallas_call(activate_kernel, out_shape=vmem(shape), in_specs=[stays()]...  1.79 us
  transfers between devices with their start and end apart: 6, of which 3 were waited for; matrix products, arithmetic and copies ran while one was open for 0% of the time, Pallas kernels for 9%

profile of v5, /device:TPU:56, one launch (start us, length us, event | category | flops | bytes accessed | tf_op | source)
XLA Modules:
  0.0 86.9 jit_solution(6804765859837643378)
XLA Ops:
  0.0 1.8 %activate.1 = bf16[4,4,32,896]{3,2,1,0:T(8,128)(2,1)S(1)} custom-call(bf16[32,14336]{1,0:T(8,128)(2,1)} %gate_ref.1, bf16[32,14336]{1,0:T(8,128)(2,1)} %up_ref.1), custom_call_target="tpu_custom_call" | custom-call | tf_op jit(solution)/shard_map/activate/pallas_call | solution.py:94
  1.8 14.3 %all_to_all.10.came = bf16[4,4,32,896]{3,2,1,0:T(8,128)(2,1)S(1)} all-to-all(bf16[4,4,32,896]{3,2,1,0:T(8,128)(2,1)S(1)} %activate.1), channel_id=1, replica_groups={{1,2,5,6},{3,0,7,4},{9,10,13,14},{11,8,15,12},{20,21,24,25},{22,23,26,2..., dimensions={0} | all-to-all | bytes 1835008 | tf_op jit(solution)/shard_map/all_to_all | solution.py:37
  16.1 0.1 regroup.1
  16.2 17.0 %collective-permute-start = (bf16[128,896]{1,0:T(8,128)(2,1)S(1)}, bf16[128,896]{1,0:T(8,128)(2,1)S(1)}, u32[]{:S(2)}, u32[]{:S(2)}) collective-permute-start(bf16[128,896]{1,0:T(8,128)(2,1)S(1)} %get-tuple-element.12), channel_id=1, source_target_pairs={{4,9},{5,8},{8,5},{9,4},{6,11},{7,10},{10,7},{11,6},{12,257},{13,2... | collective-permute-start | bytes 688136 | tf_op jit(solution)/shard_map/ppermute | solution.py:202
  33.2 2.8 %collective-permute-start.2 = (bf16[128,896]{1,0:T(8,128)(2,1)S(1)}, bf16[128,896]{1,0:T(8,128)(2,1)S(1)}, u32[]{:S(2)}, u32[]{:S(2)}) collective-permute-start(bf16[128,896]{1,0:T(8,128)(2,1)S(1)} %get-tuple-element.15), channel_id=1, source_target_pairs={{4,5},{5,4},{8,9},{9,8},{6,7},{7,6},{10,11},{11,10},{12,13},{13,12... | collective-permute-start | bytes 688136 | tf_op jit(solution)/shard_map/ppermute | solution.py:202
  36.0 1.9 %collective-permute-start.1 = (bf16[128,896]{1,0:T(8,128)(2,1)S(1)}, bf16[128,896]{1,0:T(8,128)(2,1)S(1)}, u32[]{:S(2)}, u32[]{:S(2)}) collective-permute-start(bf16[128,896]{1,0:T(8,128)(2,1)S(1)} %get-tuple-element.14), channel_id=1, source_target_pairs={{4,8},{5,9},{8,4},{9,5},{6,10},{7,11},{10,6},{11,7},{12,256},{13,2... | collective-permute-start | bytes 688136 | tf_op jit(solution)/shard_map/ppermute | solution.py:202
  37.9 0.0 collective-permute-done.rows
  37.9 3.8 %first_terms.1 = (bf16[896,4096]{1,0:T(8,128)(2,1)S(1)}, bf16[128,4096]{1,0:T(8,128)(2,1)S(1)}) custom-call(bf16[128,896]{1,0:T(8,128)(2,1)S(1)} %collective-permute-done.rows, bf16[896,4096]{1,0:T(8,128)(2,1)} %weight.1), custom_call_target="tpu_custom_call" | custom-call | flops 1 | bytes 1 | tf_op jit(solution)/shard_map/first_terms/pallas_call | solution.py:161
  41.7 5.7 %collective-permute-start.3 = (bf16[128,4096]{1,0:T(8,128)(2,1)S(1)}, bf16[128,4096]{1,0:T(8,128)(2,1)S(1)}, u32[]{:S(2)}, u32[]{:S(2)}) collective-permute-start(bf16[128,4096]{1,0:T(8,128)(2,1)S(1)} %get-tuple-element.16.earlier), channel_id=1, source_target_pairs={{4,9},{5,8},{8,5},{9,4},{6,11},{7,10},{10,7},{11,6},{12,257},{13,2... | collective-permute-start | bytes 3145736 | tf_op jit(solution)/shard_map/ppermute | solution.py:202
  47.4 0.0 collective-permute-done.2.rows
  47.4 1.3 %terms.3.earlier = bf16[128,4096]{1,0:T(8,128)(2,1)S(1)} custom-call(bf16[128,896]{1,0:T(8,128)(2,1)S(1)} %collective-permute-done.2.rows, bf16[896,4096]{1,0:T(8,128)(2,1)S(1)} %get-tuple-element.13.held, bf16[128,4096]{1,0:T(8,128)(2,1)S(1)} %get-tuple-element.16.earlier), custom_call_target="tpu_custom_call" | custom-call | flops 1 | bytes 1 | tf_op jit(solution)/shard_map/terms/pallas_call | solution.py:183
  48.7 0.0 collective-permute-done.1.rows
  48.7 1.3 %terms.4.earlier = bf16[128,4096]{1,0:T(8,128)(2,1)S(1)} custom-call(bf16[128,896]{1,0:T(8,128)(2,1)S(1)} %collective-permute-done.1.rows, bf16[896,4096]{1,0:T(8,128)(2,1)S(1)} %get-tuple-element.13.held, bf16[128,4096]{1,0:T(8,128)(2,1)S(1)} %terms.3.earlier), custom_call_target="tpu_custom_call" | custom-call | flops 1 | bytes 1 | tf_op jit(solution)/shard_map/terms/pallas_call | solution.py:183
  50.0 1.9 %collective-permute-start.5 = (bf16[128,4096]{1,0:T(8,128)(2,1)S(1)}, bf16[128,4096]{1,0:T(8,128)(2,1)S(1)}, u32[]{:S(2)}, u32[]{:S(2)}) collective-permute-start(bf16[128,4096]{1,0:T(8,128)(2,1)S(1)} %terms.4.earlier), channel_id=1, source_target_pairs={{4,8},{5,9},{8,4},{9,5},{6,10},{7,11},{10,6},{11,7},{12,256},{13,2... | collective-permute-start | bytes 3145736 | tf_op jit(solution)/shard_map/ppermute | solution.py:202
  51.9 2.8 %collective-permute-start.4 = (bf16[128,4096]{1,0:T(8,128)(2,1)S(1)}, bf16[128,4096]{1,0:T(8,128)(2,1)S(1)}, u32[]{:S(2)}, u32[]{:S(2)}) collective-permute-start(bf16[128,4096]{1,0:T(8,128)(2,1)S(1)} %terms.3.earlier), channel_id=1, source_target_pairs={{4,5},{5,4},{8,9},{9,8},{6,7},{7,6},{10,11},{11,10},{12,13},{13,12... | collective-permute-start | bytes 3145736 | tf_op jit(solution)/shard_map/ppermute | solution.py:202
  54.8 1.3 %terms.5.refs_0_ = bf16[128,4096]{1,0:T(8,128)(2,1)S(1)} custom-call(bf16[128,896]{1,0:T(8,128)(2,1)S(1)} %get-tuple-element.11.rows, bf16[896,4096]{1,0:T(8,128)(2,1)S(1)} %get-tuple-element.13.held, bf16[128,4096]{1,0:T(8,128)(2,1)S(1)} %terms.4.earlier), custom_call_target="tpu_custom_call" | custom-call | flops 1 | bytes 1 | tf_op jit(solution)/shard_map/terms/pallas_call | solution.py:183
  56.0 4.6 %collective-permute-done.3.refs_1_ = bf16[128,4096]{1,0:T(8,128)(2,1)S(1)} collective-permute-done((bf16[128,4096]{1,0:T(8,128)(2,1)S(1)}, bf16[128,4096]{1,0:T(8,128)(2,1)S(1)}, u32[]{:S(2)}, u32[]{:S(2)}) %collective-permute-start.3) | collective-permute-done | bytes 1048608 | tf_op jit(solution)/shard_map/ppermute | solution.py:202
  60.6 0.2 add.2.refs_0_
  60.9 10.6 %collective-permute-done.5.refs_2_ = bf16[128,4096]{1,0:T(8,128)(2,1)S(1)} collective-permute-done((bf16[128,4096]{1,0:T(8,128)(2,1)S(1)}, bf16[128,4096]{1,0:T(8,128)(2,1)S(1)}, u32[]{:S(2)}, u32[]{:S(2)}) %collective-permute-start.5) | collective-permute-done | bytes 1048608 | tf_op jit(solution)/shard_map/ppermute | solution.py:202
  71.5 0.3 collective-permute-done.4.refs_1_
  71.8 0.4 add.3
  72.1 13.9 %all_to_all.11.parts = bf16[4,32,4096]{2,1,0:T(8,128)(2,1)S(1)} all-to-all(bf16[4,32,4096]{2,1,0:T(8,128)(2,1)S(1)} %bitcast.1), channel_id=1, replica_groups={{1,2,5,6},{3,0,7,4},{9,10,13,14},{11,8,15,12},{20,21,24,25},{22,23,26,2..., dimensions={0} | all-to-all | bytes 2097152 | tf_op jit(solution)/shard_map/all_to_all | solution.py:37
  86.0 0.8 outer_sum.1
Async XLA Ops:
  16.2 21.7 %collective-permute-start = (bf16[128,896]{1,0:T(8,128)(2,1)S(1)}, bf16[128,896]{1,0:T(8,128)(2,1)S(1)}, u32[]{:S(2)}, u32[]{:S(2)}) collective-permute-start(bf16[128,896]{1,0:T(8,128)(2,1)S(1)} %get-tuple-element.12), channel_id=1, source_target_pairs={{4,9},{5,8},{8,5},{9,4},{6,11},{7,10},{10,7},{11,6},{12,257},{13,2... | collective-permute-start | bytes 688136 | tf_op jit(solution)/shard_map/ppermute | solution.py:202
  33.2 14.2 %collective-permute-start.2 = (bf16[128,896]{1,0:T(8,128)(2,1)S(1)}, bf16[128,896]{1,0:T(8,128)(2,1)S(1)}, u32[]{:S(2)}, u32[]{:S(2)}) collective-permute-start(bf16[128,896]{1,0:T(8,128)(2,1)S(1)} %get-tuple-element.15), channel_id=1, source_target_pairs={{4,5},{5,4},{8,9},{9,8},{6,7},{7,6},{10,11},{11,10},{12,13},{13,12... | collective-permute-start | bytes 688136 | tf_op jit(solution)/shard_map/ppermute | solution.py:202
  36.0 12.7 %collective-permute-start.1 = (bf16[128,896]{1,0:T(8,128)(2,1)S(1)}, bf16[128,896]{1,0:T(8,128)(2,1)S(1)}, u32[]{:S(2)}, u32[]{:S(2)}) collective-permute-start(bf16[128,896]{1,0:T(8,128)(2,1)S(1)} %get-tuple-element.14), channel_id=1, source_target_pairs={{4,8},{5,9},{8,4},{9,5},{6,10},{7,11},{10,6},{11,7},{12,256},{13,2... | collective-permute-start | bytes 688136 | tf_op jit(solution)/shard_map/ppermute | solution.py:202
  41.7 18.9 %collective-permute-start.3 = (bf16[128,4096]{1,0:T(8,128)(2,1)S(1)}, bf16[128,4096]{1,0:T(8,128)(2,1)S(1)}, u32[]{:S(2)}, u32[]{:S(2)}) collective-permute-start(bf16[128,4096]{1,0:T(8,128)(2,1)S(1)} %get-tuple-element.16.earlier), channel_id=1, source_target_pairs={{4,9},{5,8},{8,5},{9,4},{6,11},{7,10},{10,7},{11,6},{12,257},{13,2... | collective-permute-start | bytes 3145736 | tf_op jit(solution)/shard_map/ppermute | solution.py:202
  50.0 21.5 %collective-permute-start.5 = (bf16[128,4096]{1,0:T(8,128)(2,1)S(1)}, bf16[128,4096]{1,0:T(8,128)(2,1)S(1)}, u32[]{:S(2)}, u32[]{:S(2)}) collective-permute-start(bf16[128,4096]{1,0:T(8,128)(2,1)S(1)} %terms.4.earlier), channel_id=1, source_target_pairs={{4,8},{5,9},{8,4},{9,5},{6,10},{7,11},{10,6},{11,7},{12,256},{13,2... | collective-permute-start | bytes 3145736 | tf_op jit(solution)/shard_map/ppermute | solution.py:202
  51.9 19.8 %collective-permute-start.4 = (bf16[128,4096]{1,0:T(8,128)(2,1)S(1)}, bf16[128,4096]{1,0:T(8,128)(2,1)S(1)}, u32[]{:S(2)}, u32[]{:S(2)}) collective-permute-start(bf16[128,4096]{1,0:T(8,128)(2,1)S(1)} %terms.3.earlier), channel_id=1, source_target_pairs={{4,5},{5,4},{8,9},{9,8},{6,7},{7,6},{10,11},{11,10},{12,13},{13,12... | collective-permute-start | bytes 3145736 | tf_op jit(solution)/shard_map/ppermute | solution.py:202

commit v6 on v5

--- a/solution.py
+++ b/solution.py
@@ -67,26 +67,30 @@
     def member(value, shift, bit):
         return lax.div(value + shift, 2) * 2 - shift + bit
 
-    copies = []
-    for i, (oz, ox) in enumerate(BITS):
-        for j, (iz, ix) in enumerate(BITS):
-            to_z = member(member(zl + 4, core, oz), 1 - core, iz)
-            to_x = member(member(x + 4, 1 - core, ox), core, ix)
-            block = lax.rem(to_z, Z_LO) * X + lax.rem(to_x, X)
-            columns = pl.ds(pl.multiple_of(block * WIDTH, 128), WIDTH)
+    slabs, copies = [], []
+    for oz in range(2):
+        for iz in range(2):
+            slab = lax.rem(member(member(zl + 4, core, oz), 1 - core, iz), Z_LO)
+            columns = pl.ds(pl.multiple_of(slab * X * WIDTH, 128), X * WIDTH)
+            place = 2 * oz + iz
             pair = (
-                pltpu.make_async_copy(gate_ref.at[:, columns], gate_buf.at[i, j], sems.at[0, i, j]),
-                pltpu.make_async_copy(up_ref.at[:, columns], up_buf.at[i, j], sems.at[1, i, j]),
+                pltpu.make_async_copy(gate_ref.at[:, columns], gate_buf.at[place], sems.at[0, place]),
+                pltpu.make_async_copy(up_ref.at[:, columns], up_buf.at[place], sems.at[1, place]),
             )
             for copy in pair:
                 copy.start()
+            slabs.append((oz, iz))
             copies.append(pair)
-    for i in range(4):
-        for j in range(4):
-            for copy in copies[4 * i + j]:
-                copy.wait()
-            gate = gate_buf[i, j].astype(jnp.float32)
-            out[i, j] = (jax.nn.silu(gate) * up_buf[i, j].astype(jnp.float32)).astype(jnp.bfloat16)
+    for place, (oz, iz) in enumerate(slabs):
+        for copy in copies[place]:
+            copy.wait()
+        for ox in range(2):
+            for ix in range(2):
+                block = lax.rem(member(member(x + 4, 1 - core, ox), core, ix), X)
+                columns = pl.ds(pl.multiple_of(block * WIDTH, 128), WIDTH)
+                gate = gate_buf[place, :, columns].astype(jnp.float32)
+                up = up_buf[place, :, columns].astype(jnp.float32)
+                out[2 * oz + ox, 2 * iz + ix] = (jax.nn.silu(gate) * up).astype(jnp.bfloat16)
 
 
 def activate(gate_pre, up_pre):
@@ -97,9 +101,9 @@
         in_specs=[stays()] * 2,
         out_specs=whole(),
         scratch_shapes=[
-            pltpu.VMEM(shape, jnp.bfloat16),
-            pltpu.VMEM(shape, jnp.bfloat16),
-            pltpu.SemaphoreType.DMA((2, 4, 4)),
+            pltpu.VMEM((4, ROWS, X * WIDTH), jnp.bfloat16),
+            pltpu.VMEM((4, ROWS, X * WIDTH), jnp.bfloat16),
+            pltpu.SemaphoreType.DMA((2, 4)),
         ],
         compiler_params=pltpu.CompilerParams(vmem_limit_bytes=8 * MIB),
         name="activate",
@@ -226,13 +230,21 @@
     )(*(in_vmem(part) for part in parts))
 
 
-def outer_sum_kernel(parts, out):
-    for tile in range(TILES):
-        columns = slice(TILE * tile, TILE * (tile + 1))
-        total = parts[0, :, columns].astype(jnp.float32)
-        for member in range(1, 4):
-            total += parts[member, :, columns].astype(jnp.float32)
-        out[:, columns] = total.astype(jnp.bfloat16)
+def outer_sum_kernel(parts, out, total, sems):
+    half = D // 2
+    copies = []
+    for side in range(2):
+        for tile in range(TILES // 2):
+            columns = slice(half * side + TILE * tile, half * side + TILE * (tile + 1))
+            terms = parts[0, :, columns].astype(jnp.float32)
+            for member in range(1, 4):
+                terms += parts[member, :, columns].astype(jnp.float32)
+            total[:, columns] = terms.astype(jnp.bfloat16)
+        columns = slice(half * side, half * (side + 1))
+        copies.append(pltpu.make_async_copy(total.at[:, columns], out.at[:, columns], sems.at[side]))
+        copies[-1].start()
+    for copy in copies:
+        copy.wait()
 
 
 def outer_sum(parts):
@@ -240,7 +252,8 @@
         outer_sum_kernel,
         out_shape=jax.ShapeDtypeStruct((ROWS, D), jnp.bfloat16),
         in_specs=[whole()],
-        out_specs=whole(),
+        out_specs=pl.BlockSpec(memory_space=pltpu.HBM),
+        scratch_shapes=[pltpu.VMEM((ROWS, D), jnp.bfloat16), pltpu.SemaphoreType.DMA((2,))],
         compiler_params=pltpu.CompilerParams(vmem_limit_bytes=4 * MIB),
         name="outer_sum",
     )(in_vmem(parts))

time: 87.3 us -> 87.1 us (level)
  no operation moved by 1% of the time
where the time goes in v6:
time: 87.1 us; the launch traced here: 86.8 us
  starting transfers between devices  32.1 us (37%)
  blocking collectives  28.2 us (32%)
  waiting for transfers between devices  15.5 us (18%)
  Pallas kernels  10.8 us (12%)
    ppermute x6, starting transfers between devices, trade(): return lax.ppermute(value, AXES, partners(flipped))  32.1 us
    all_to_all x2, blocking collectives, swap(): lax.all_to_all(value, AXES, split_axis=0, concat_axis=0, axis_index_group...  28.2 us
    ppermute x6, waiting for transfers between devices, trade(): return lax.ppermute(value, AXES, partners(flipped))  15.5 us
    pallas_call x3, Pallas kernels, terms_for(): pl.pallas_call(terms_kernel, out_shape=vmem((4 * ROWS, D)), in_specs=[who...  3.83 us
    pallas_call x1, Pallas kernels, first_terms(): pl.pallas_call(first_terms_kernel, out_shape=[vmem((WIDTH, D)), vmem((4 *...  3.77 us
  transfers between devices with their start and end apart: 6, of which 3 were waited for; matrix products, arithmetic and copies ran while one was open for 0% of the time, Pallas kernels for 9%

profile of v6, /device:TPU:56, one launch (start us, length us, event | category | flops | bytes accessed | tf_op | source)
XLA Modules:
  0.0 86.8 jit_solution(7025446027869436421)
XLA Ops:
  0.0 1.7 %activate.1 = bf16[4,4,32,896]{3,2,1,0:T(8,128)(2,1)S(1)} custom-call(bf16[32,14336]{1,0:T(8,128)(2,1)} %gate_ref.1, bf16[32,14336]{1,0:T(8,128)(2,1)} %up_ref.1), custom_call_target="tpu_custom_call" | custom-call | tf_op jit(solution)/shard_map/activate/pallas_call | solution.py:98
  1.7 14.3 %all_to_all.10.came = bf16[4,4,32,896]{3,2,1,0:T(8,128)(2,1)S(1)} all-to-all(bf16[4,4,32,896]{3,2,1,0:T(8,128)(2,1)S(1)} %activate.1), channel_id=1, replica_groups={{1,2,5,6},{3,0,7,4},{9,10,13,14},{11,8,15,12},{20,21,24,25},{22,23,26,2..., dimensions={0} | all-to-all | bytes 1835008 | tf_op jit(solution)/shard_map/all_to_all | solution.py:37
  16.1 0.1 regroup.1
  16.1 17.0 %collective-permute-start = (bf16[128,896]{1,0:T(8,128)(2,1)S(1)}, bf16[128,896]{1,0:T(8,128)(2,1)S(1)}, u32[]{:S(2)}, u32[]{:S(2)}) collective-permute-start(bf16[128,896]{1,0:T(8,128)(2,1)S(1)} %get-tuple-element.12), channel_id=1, source_target_pairs={{4,9},{5,8},{8,5},{9,4},{6,11},{7,10},{10,7},{11,6},{12,257},{13,2... | collective-permute-start | bytes 688136 | tf_op jit(solution)/shard_map/ppermute | solution.py:206
  33.1 2.8 %collective-permute-start.2 = (bf16[128,896]{1,0:T(8,128)(2,1)S(1)}, bf16[128,896]{1,0:T(8,128)(2,1)S(1)}, u32[]{:S(2)}, u32[]{:S(2)}) collective-permute-start(bf16[128,896]{1,0:T(8,128)(2,1)S(1)} %get-tuple-element.15), channel_id=1, source_target_pairs={{4,5},{5,4},{8,9},{9,8},{6,7},{7,6},{10,11},{11,10},{12,13},{13,12... | collective-permute-start | bytes 688136 | tf_op jit(solution)/shard_map/ppermute | solution.py:206
  35.9 1.9 %collective-permute-start.1 = (bf16[128,896]{1,0:T(8,128)(2,1)S(1)}, bf16[128,896]{1,0:T(8,128)(2,1)S(1)}, u32[]{:S(2)}, u32[]{:S(2)}) collective-permute-start(bf16[128,896]{1,0:T(8,128)(2,1)S(1)} %get-tuple-element.14), channel_id=1, source_target_pairs={{4,8},{5,9},{8,4},{9,5},{6,10},{7,11},{10,6},{11,7},{12,256},{13,2... | collective-permute-start | bytes 688136 | tf_op jit(solution)/shard_map/ppermute | solution.py:206
  37.9 0.0 collective-permute-done.rows
  37.9 3.8 %first_terms.1 = (bf16[896,4096]{1,0:T(8,128)(2,1)S(1)}, bf16[128,4096]{1,0:T(8,128)(2,1)S(1)}) custom-call(bf16[128,896]{1,0:T(8,128)(2,1)S(1)} %collective-permute-done.rows, bf16[896,4096]{1,0:T(8,128)(2,1)} %weight.1), custom_call_target="tpu_custom_call" | custom-call | flops 1 | bytes 1 | tf_op jit(solution)/shard_map/first_terms/pallas_call | solution.py:165
  41.7 5.7 %collective-permute-start.3 = (bf16[128,4096]{1,0:T(8,128)(2,1)S(1)}, bf16[128,4096]{1,0:T(8,128)(2,1)S(1)}, u32[]{:S(2)}, u32[]{:S(2)}) collective-permute-start(bf16[128,4096]{1,0:T(8,128)(2,1)S(1)} %get-tuple-element.16.earlier), channel_id=1, source_target_pairs={{4,9},{5,8},{8,5},{9,4},{6,11},{7,10},{10,7},{11,6},{12,257},{13,2... | collective-permute-start | bytes 3145736 | tf_op jit(solution)/shard_map/ppermute | solution.py:206
  47.3 0.0 collective-permute-done.2.rows
  47.4 1.3 %terms.3.earlier = bf16[128,4096]{1,0:T(8,128)(2,1)S(1)} custom-call(bf16[128,896]{1,0:T(8,128)(2,1)S(1)} %collective-permute-done.2.rows, bf16[896,4096]{1,0:T(8,128)(2,1)S(1)} %get-tuple-element.13.held, bf16[128,4096]{1,0:T(8,128)(2,1)S(1)} %get-tuple-element.16.earlier), custom_call_target="tpu_custom_call" | custom-call | flops 1 | bytes 1 | tf_op jit(solution)/shard_map/terms/pallas_call | solution.py:187
  48.6 0.0 collective-permute-done.1.rows
  48.6 1.3 %terms.4.earlier = bf16[128,4096]{1,0:T(8,128)(2,1)S(1)} custom-call(bf16[128,896]{1,0:T(8,128)(2,1)S(1)} %collective-permute-done.1.rows, bf16[896,4096]{1,0:T(8,128)(2,1)S(1)} %get-tuple-element.13.held, bf16[128,4096]{1,0:T(8,128)(2,1)S(1)} %terms.3.earlier), custom_call_target="tpu_custom_call" | custom-call | flops 1 | bytes 1 | tf_op jit(solution)/shard_map/terms/pallas_call | solution.py:187
  49.9 1.9 %collective-permute-start.5 = (bf16[128,4096]{1,0:T(8,128)(2,1)S(1)}, bf16[128,4096]{1,0:T(8,128)(2,1)S(1)}, u32[]{:S(2)}, u32[]{:S(2)}) collective-permute-start(bf16[128,4096]{1,0:T(8,128)(2,1)S(1)} %terms.4.earlier), channel_id=1, source_target_pairs={{4,8},{5,9},{8,4},{9,5},{6,10},{7,11},{10,6},{11,7},{12,256},{13,2... | collective-permute-start | bytes 3145736 | tf_op jit(solution)/shard_map/ppermute | solution.py:206
  51.9 2.8 %collective-permute-start.4 = (bf16[128,4096]{1,0:T(8,128)(2,1)S(1)}, bf16[128,4096]{1,0:T(8,128)(2,1)S(1)}, u32[]{:S(2)}, u32[]{:S(2)}) collective-permute-start(bf16[128,4096]{1,0:T(8,128)(2,1)S(1)} %terms.3.earlier), channel_id=1, source_target_pairs={{4,5},{5,4},{8,9},{9,8},{6,7},{7,6},{10,11},{11,10},{12,13},{13,12... | collective-permute-start | bytes 3145736 | tf_op jit(solution)/shard_map/ppermute | solution.py:206
  54.7 1.3 %terms.5.refs_0_ = bf16[128,4096]{1,0:T(8,128)(2,1)S(1)} custom-call(bf16[128,896]{1,0:T(8,128)(2,1)S(1)} %get-tuple-element.11.rows, bf16[896,4096]{1,0:T(8,128)(2,1)S(1)} %get-tuple-element.13.held, bf16[128,4096]{1,0:T(8,128)(2,1)S(1)} %terms.4.earlier), custom_call_target="tpu_custom_call" | custom-call | flops 1 | bytes 1 | tf_op jit(solution)/shard_map/terms/pallas_call | solution.py:187
  56.0 4.6 %collective-permute-done.3.refs_1_ = bf16[128,4096]{1,0:T(8,128)(2,1)S(1)} collective-permute-done((bf16[128,4096]{1,0:T(8,128)(2,1)S(1)}, bf16[128,4096]{1,0:T(8,128)(2,1)S(1)}, u32[]{:S(2)}, u32[]{:S(2)}) %collective-permute-start.3) | collective-permute-done | bytes 1048608 | tf_op jit(solution)/shard_map/ppermute | solution.py:206
  60.6 0.2 add.2.refs_0_
  60.8 10.6 %collective-permute-done.5.refs_2_ = bf16[128,4096]{1,0:T(8,128)(2,1)S(1)} collective-permute-done((bf16[128,4096]{1,0:T(8,128)(2,1)S(1)}, bf16[128,4096]{1,0:T(8,128)(2,1)S(1)}, u32[]{:S(2)}, u32[]{:S(2)}) %collective-permute-start.5) | collective-permute-done | bytes 1048608 | tf_op jit(solution)/shard_map/ppermute | solution.py:206
  71.4 0.3 collective-permute-done.4.refs_1_
  71.7 0.4 add.3
  72.1 13.9 %all_to_all.11.parts = bf16[4,32,4096]{2,1,0:T(8,128)(2,1)S(1)} all-to-all(bf16[4,32,4096]{2,1,0:T(8,128)(2,1)S(1)} %bitcast.1), channel_id=1, replica_groups={{1,2,5,6},{3,0,7,4},{9,10,13,14},{11,8,15,12},{20,21,24,25},{22,23,26,2..., dimensions={0} | all-to-all | bytes 2097152 | tf_op jit(solution)/shard_map/all_to_all | solution.py:37
  86.0 0.8 outer_sum.1
Async XLA Ops:
  16.1 21.7 %collective-permute-start = (bf16[128,896]{1,0:T(8,128)(2,1)S(1)}, bf16[128,896]{1,0:T(8,128)(2,1)S(1)}, u32[]{:S(2)}, u32[]{:S(2)}) collective-permute-start(bf16[128,896]{1,0:T(8,128)(2,1)S(1)} %get-tuple-element.12), channel_id=1, source_target_pairs={{4,9},{5,8},{8,5},{9,4},{6,11},{7,10},{10,7},{11,6},{12,257},{13,2... | collective-permute-start | bytes 688136 | tf_op jit(solution)/shard_map/ppermute | solution.py:206
  33.1 14.2 %collective-permute-start.2 = (bf16[128,896]{1,0:T(8,128)(2,1)S(1)}, bf16[128,896]{1,0:T(8,128)(2,1)S(1)}, u32[]{:S(2)}, u32[]{:S(2)}) collective-permute-start(bf16[128,896]{1,0:T(8,128)(2,1)S(1)} %get-tuple-element.15), channel_id=1, source_target_pairs={{4,5},{5,4},{8,9},{9,8},{6,7},{7,6},{10,11},{11,10},{12,13},{13,12... | collective-permute-start | bytes 688136 | tf_op jit(solution)/shard_map/ppermute | solution.py:206
  35.9 12.7 %collective-permute-start.1 = (bf16[128,896]{1,0:T(8,128)(2,1)S(1)}, bf16[128,896]{1,0:T(8,128)(2,1)S(1)}, u32[]{:S(2)}, u32[]{:S(2)}) collective-permute-start(bf16[128,896]{1,0:T(8,128)(2,1)S(1)} %get-tuple-element.14), channel_id=1, source_target_pairs={{4,8},{5,9},{8,4},{9,5},{6,10},{7,11},{10,6},{11,7},{12,256},{13,2... | collective-permute-start | bytes 688136 | tf_op jit(solution)/shard_map/ppermute | solution.py:206
  41.7 18.9 %collective-permute-start.3 = (bf16[128,4096]{1,0:T(8,128)(2,1)S(1)}, bf16[128,4096]{1,0:T(8,128)(2,1)S(1)}, u32[]{:S(2)}, u32[]{:S(2)}) collective-permute-start(bf16[128,4096]{1,0:T(8,128)(2,1)S(1)} %get-tuple-element.16.earlier), channel_id=1, source_target_pairs={{4,9},{5,8},{8,5},{9,4},{6,11},{7,10},{10,7},{11,6},{12,257},{13,2... | collective-permute-start | bytes 3145736 | tf_op jit(solution)/shard_map/ppermute | solution.py:206
  49.9 21.5 %collective-permute-start.5 = (bf16[128,4096]{1,0:T(8,128)(2,1)S(1)}, bf16[128,4096]{1,0:T(8,128)(2,1)S(1)}, u32[]{:S(2)}, u32[]{:S(2)}) collective-permute-start(bf16[128,4096]{1,0:T(8,128)(2,1)S(1)} %terms.4.earlier), channel_id=1, source_target_pairs={{4,8},{5,9},{8,4},{9,5},{6,10},{7,11},{10,6},{11,7},{12,256},{13,2... | collective-permute-start | bytes 3145736 | tf_op jit(solution)/shard_map/ppermute | solution.py:206
  51.9 19.8 %collective-permute-start.4 = (bf16[128,4096]{1,0:T(8,128)(2,1)S(1)}, bf16[128,4096]{1,0:T(8,128)(2,1)S(1)}, u32[]{:S(2)}, u32[]{:S(2)}) collective-permute-start(bf16[128,4096]{1,0:T(8,128)(2,1)S(1)} %terms.3.earlier), channel_id=1, source_target_pairs={{4,5},{5,4},{8,9},{9,8},{6,7},{7,6},{10,11},{11,10},{12,13},{13,12... | collective-permute-start | bytes 3145736 | tf_op jit(solution)/shard_map/ppermute | solution.py:206
